TPU v7x, 128 devices: a whole 4x4x4 slice. The times are simulated.
128 devices in a mesh: gx: 8 (over x, core), gy: 4 (over z), gz: 4 (over y).
Axes of the slice: x: 4, y: 4, z: 4, core: 2. Of those that a mesh axis runs over, the one named last changes fastest.
Arguments:
- right_side: float32 [2048, 128], P(('gx', 'gy', 'gz')), may hold values from -53 to 53
- diagonal: float32 [2048, 128], P(('gx', 'gy', 'gz')), may hold values from 0.5 to 2
- near_blocks: bfloat16 [24576, 128, 128], P(('gx', 'gy', 'gz')), may hold values from -0.109375 to 0.109375
- near_rows: int32 [24576], P(('gx', 'gy', 'gz')), may hold values from 0 to 2047, as said below
- near_cols: int32 [24576], P(('gx', 'gy', 'gz')), may hold values from 0 to 2047, as said below
- near_count: int32 [128], P(('gx', 'gy', 'gz')), may hold values from 16 to 192, as said below
- basis: bfloat16 [2048, 32, 128], P(('gx', 'gy', 'gz')), may hold values from -0.5 to 0.5
- coupling: bfloat16 [65536, 1024], P(('gx', 'gy', 'gz')), may hold values from -0.41992188 to 0.41992188
- far_rows: int32 [65536], P(('gx', 'gy', 'gz')), may hold values from 0 to 2047, as said below
- far_cols: int32 [65536], P(('gx', 'gy', 'gz')), may hold values from 0 to 2047, as said below
- far_rank: int32 [65536], P(('gx', 'gy', 'gz')), may hold values from 4 to 32, as said below
Outputs:
- solution: float32 [2048, 128], P(('gx', 'gy', 'gz'))
- residual: float32 [2048, 128], P(('gx', 'gy', 'gz'))
Inputs may be any that keep to these rules, and one draw needn't show every extreme that they name: `near_rows`: each slot names a cluster of the device that holds the slot, device g holding clusters g * 16 to g * 16 + 15; the first 16 slots of a device name its clusters in order. `near_cols`: each slot names a cluster of the device that holds it or of the device just before or after it in the order of gx, gy, gz; the first 16 slots of a device repeat their row cluster. `near_count`: slots at or after a device's count are unused; some device uses all 192. `far_rows`: each slot names a cluster of the device that holds the slot. `far_cols`: of the slots of one device, at most 8 name clusters of any one device, and on every device exactly 8 name clusters of some one device. `far_rank`: the first slot of every device has rank 32.
All inputs are finite; a program needn't handle non-finite values.
Results may differ from a plain program's by a relative error of at most 0.0023.
Values may be sent and summed in bfloat16 or wider, within the bound.
A program may use at most 128 MiB of HBM per device.

v0:
```python
import jax
import jax.numpy as jnp
from jax import lax
from jax.sharding import PartitionSpec as P

ITERS = 3


epsilon = 1e-06


def extended(array, sides, width):
    for axis, dim in sides:
        devices, length = (lax.axis_size(axis), array.shape[dim])
        up = [(i, (i + 1) % devices) for i in range(devices - 1)]
        down = [(j, i) for i, j in up]
        last = lax.slice_in_dim(array, length - width, length, axis=dim)
        initial = lax.slice_in_dim(array, 0, width, axis=dim)
        before = lax.ppermute(last, axis, up)
        after = lax.ppermute(initial, axis, down)
        array = jnp.concatenate([before, array, after], axis=dim)
    return array


def on_device(
    right_side,
    diagonal,
    near_blocks,
    near_rows,
    near_cols,
    near_count,
    basis,
    coupling,
    far_rows,
    far_cols,
    far_rank,
):
    groups = lax.axis_size(("gx", "gy", "gz"))
    device = lax.axis_index(("gx", "gy", "gz"))
    per_device = right_side.shape[0]
    rank_top = basis.shape[1]
    near_slots = near_blocks.shape[0]
    far_slots = coupling.shape[0]
    total_clusters = per_device * groups
    live_slot = (jnp.arange(near_slots, dtype=jnp.int32) < near_count[0]).astype(jnp.float32)[
        :, None
    ]
    row_local = near_rows - device * per_device
    col_local = near_cols - (device - 1) * per_device
    near_row_hot = (row_local[:, None] == jnp.arange(per_device, dtype=jnp.int32)[None, :]).astype(
        jnp.float32
    )
    near_col_hot = (
        col_local[:, None] == jnp.arange(3 * per_device, dtype=jnp.int32)[None, :]
    ).astype(jnp.float32)
    far_local = far_rows - device * per_device
    far_row_hot = (far_local[:, None] == jnp.arange(per_device, dtype=jnp.int32)[None, :]).astype(
        jnp.float32
    )
    levels = jnp.arange(rank_top, dtype=jnp.int32)
    rank_mask = (levels[None, :, None] < far_rank[:, None, None]) & (
        levels[None, None, :] < far_rank[:, None, None]
    )
    coupled = jnp.where(
        rank_mask,
        coupling.reshape(far_slots, rank_top, rank_top).astype(jnp.float32),
        jnp.float32(0.0),
    )
    solution = jnp.zeros_like(right_side)
    residual = right_side
    for sweep in range(ITERS):
        field_low = residual.astype(jnp.bfloat16)
        window = extended(field_low, ((("gx", "gy", "gz"), 0),), per_device)
        forward = (
            jnp.einsum(
                "kab,kb->ka",
                near_blocks,
                jnp.take(window, col_local, axis=0),
                preferred_element_type=jnp.float32,
            )
            * live_slot
        )
        backward = (
            jnp.einsum(
                "kab,ka->kb",
                near_blocks,
                jnp.take(field_low, row_local, axis=0),
                preferred_element_type=jnp.float32,
            )
            * live_slot
        )
        near_part = jnp.einsum("kc,km->cm", near_row_hot, forward, precision=lax.Precision.HIGHEST)
        spilled = jnp.einsum("kc,km->cm", near_col_hot, backward, precision=lax.Precision.HIGHEST)
        near_part = near_part + spilled[per_device : 2 * per_device]
        outgoing = jnp.concatenate([spilled[:per_device], spilled[2 * per_device :]], axis=0)
        returned = extended(outgoing, ((("gx", "gy", "gz"), 0),), per_device)
        near_part = near_part + returned[:per_device] + returned[3 * per_device :]
        own_coeffs = jnp.einsum("crm,cm->cr", basis, field_low, preferred_element_type=jnp.float32)
        all_coeffs = lax.all_gather(own_coeffs, ("gx", "gy", "gz"), axis=0, tiled=True)
        far_forward = jnp.einsum(
            "kab,kb->ka",
            coupled,
            jnp.take(all_coeffs, far_cols, axis=0),
            precision=lax.Precision.HIGHEST,
        )
        far_backward = jnp.einsum(
            "kab,ka->kb",
            coupled,
            jnp.take(own_coeffs, far_local, axis=0),
            precision=lax.Precision.HIGHEST,
        )
        far_sum = jnp.einsum("kc,kr->cr", far_row_hot, far_forward, precision=lax.Precision.HIGHEST)
        spread = jax.ops.segment_sum(far_backward, far_cols, num_segments=total_clusters)
        arriving = lax.psum_scatter(spread, ("gx", "gy", "gz"), scatter_dimension=0, tiled=True)
        far_sum = far_sum + arriving
        far_part = jnp.einsum(
            "crm,cr->cm", basis, far_sum.astype(jnp.bfloat16), preferred_element_type=jnp.float32
        )
        image = diagonal * residual + near_part + far_part
        cross_term, square_term = lax.psum(
            (jnp.sum(residual * image), jnp.sum(image * image)), ("gx", "gy", "gz")
        )
        step_size = cross_term / (square_term + epsilon)
        solution = solution + step_size * residual
        residual = residual - step_size * image
    return (solution, residual)


def solution(mesh):
    placed = (
        P(("gx", "gy", "gz"), None),
        P(("gx", "gy", "gz"), None),
        P(("gx", "gy", "gz"), None, None),
        P(("gx", "gy", "gz")),
        P(("gx", "gy", "gz")),
        P(("gx", "gy", "gz")),
        P(("gx", "gy", "gz"), None, None),
        P(("gx", "gy", "gz"), None),
        P(("gx", "gy", "gz")),
        P(("gx", "gy", "gz")),
        P(("gx", "gy", "gz")),
    )
    return jax.shard_map(
        on_device,
        mesh=mesh,
        in_specs=placed,
        out_specs=(P(("gx", "gy", "gz"), None), P(("gx", "gy", "gz"), None)),
        check_vma=False,
    )
```

profile of v0, /device:TPU:1, one launch (start us, length us, event | category | flops | bytes accessed | tf_op | source)
XLA Modules:
  0.0 2341.8 jit_solution(16835832148686677984)
XLA Ops:
  7.2 0.7 convert_element_type.34
  8.0 9.5 collective-permute-start.1
  17.5 1.9 collective-permute-start
  19.4 0.7 convert_bitcast_fusion
  20.1 1.5 copy.13
  21.6 0.7 iota_compare_fusion.12
  22.7 7.7 copy.23
  30.6 1.0 gather_fusion.3
  31.8 15.4 fusion.78
  47.3 3.2 scatter_custom_fusion
  50.7 0.8 gather_fusion.1
  52.2 4.5 fusion.35
  57.1 7.0 collective-permute-start.3
  64.1 2.1 collective-permute-start.2
  66.2 7.6 copy.20
  73.8 59.3 %all_gather.9 = f32[2048,32]{1,0:T(8,128)S(1)} all-gather(f32[16,32]{1,0:T(8,128)S(1)} %bitcast.108), channel_id=1, replica_groups=mesh['gx'=8,'gy'=4,'gz'=4] {'gx','gy','gz'}, dimensions={0}, use_global_device_ids=true | all-gather | bytes 264192 | tf_op jit(solution)/shard_map/all_gather | solution.py:99
  133.1 1.0 gather_fusion.2
  134.4 15.4 fusion.77
  149.8 0.8 gather_fusion
  150.7 6.1 fusion.37
  156.8 500.8 %reduce-scatter.4.cloned.1.call-done = f32[16,32]{1,0:T(8,128)} async-done(((f32[2048,32]{1,0:T(8,128)}), f32[16,32]{1,0:T(8,128)}) %reduce-scatter.4.cloned.1.call-update) | async-done | bytes 2064 | tf_op jit(solution)/shard_map/reduce_scatter | solution.py:114
  657.6 1.1 fusion.17
  659.0 0.9 multiply_reduce_fusion.4
  659.9 93.6 %all-reduce.2 = (f32[]{:T(128)}, f32[]{:T(128)}) all-reduce(f32[]{:T(128)} %get-tuple-element.11, f32[]{:T(128)} %get-tuple-element.10), channel_id=1, replica_groups=mesh['gx'=8,'gy'=4,'gz'=4] {'gx','gy','gz'}, use_global_device_ids=true, to_apply=%region_3.8 | all-reduce | flops 2 | bytes 16 | tf_op jit(solution)/shard_map/psum | solution.py:120
  755.6 1.0 gather_fusion.7
  756.6 57.6 %all_gather.10 = f32[2048,32]{1,0:T(8,128)S(1)} all-gather(f32[16,32]{1,0:T(8,128)S(1)} %bitcast.112), channel_id=1, replica_groups=mesh['gx'=8,'gy'=4,'gz'=4] {'gx','gy','gz'}, dimensions={0}, use_global_device_ids=true | all-gather | bytes 264192 | tf_op jit(solution)/shard_map/all_gather | solution.py:99
  814.2 1.4 gather_fusion.5
  815.6 4.2 collective-permute-start.5
  819.8 1.9 collective-permute-start.4
  821.8 15.4 fusion.80
  837.3 3.2 scatter_custom_fusion.1
  840.8 1.3 gather_fusion.6
  842.1 0.8 broadcast_select_fusion.3
  842.9 15.6 fusion.79
  858.5 0.7 select_bitcast_fusion.2
  859.3 1.7 fusion.31
  861.4 7.0 collective-permute-start.7
  868.3 1.9 collective-permute-start.6
  871.0 0.9 gather_fusion.4
  872.0 6.1 fusion.33
  878.1 569.7 %reduce-scatter.6.cloned.1.call-done = f32[16,32]{1,0:T(8,128)} async-done(((f32[2048,32]{1,0:T(8,128)}), f32[16,32]{1,0:T(8,128)}) %reduce-scatter.6.cloned.1.call-update) | async-done | bytes 2064 | tf_op jit(solution)/shard_map/reduce_scatter | solution.py:114
  1447.8 1.1 fusion.16
  1449.1 1.0 multiply_reduce_fusion.2
  1450.1 93.9 %all-reduce.1 = (f32[]{:T(128)}, f32[]{:T(128)}) all-reduce(f32[]{:T(128)} %get-tuple-element.9, f32[]{:T(128)} %get-tuple-element.8), channel_id=1, replica_groups=mesh['gx'=8,'gy'=4,'gz'=4] {'gx','gy','gz'}, use_global_device_ids=true, to_apply=%region_9.14 | all-reduce | flops 2 | bytes 16 | tf_op jit(solution)/shard_map/psum | solution.py:120
  1546.0 1.0 gather_fusion.11
  1547.1 57.2 %all_gather.11 = f32[2048,32]{1,0:T(8,128)S(1)} all-gather(f32[16,32]{1,0:T(8,128)S(1)} %bitcast.110), channel_id=1, replica_groups=mesh['gx'=8,'gy'=4,'gz'=4] {'gx','gy','gz'}, dimensions={0}, use_global_device_ids=true | all-gather | bytes 264192 | tf_op jit(solution)/shard_map/all_gather | solution.py:99
  1604.3 1.5 gather_fusion.9
  1605.8 4.1 collective-permute-start.9
  1610.0 2.1 collective-permute-start.8
  1612.2 15.4 fusion.82
  1627.7 3.6 scatter_custom_fusion.2
  1631.3 1.3 gather_fusion.10
  1632.6 0.8 broadcast_select_fusion.1
  1633.5 15.6 fusion.81
  1649.1 0.7 select_bitcast_fusion
  1649.8 1.7 fusion.27
  1651.9 7.0 collective-permute-start.11
  1658.9 1.9 collective-permute-start.10
  1661.5 0.9 gather_fusion.8
  1662.6 6.1 fusion.29
  1668.7 568.4 %reduce-scatter.8.cloned.1.call-done = f32[16,32]{1,0:T(8,128)} async-done(((f32[2048,32]{1,0:T(8,128)}), f32[16,32]{1,0:T(8,128)}) %reduce-scatter.8.cloned.1.call-update) | async-done | bytes 2064 | tf_op jit(solution)/shard_map/reduce_scatter | solution.py:114
  2237.1 1.1 fusion.15
  2238.4 1.0 multiply_reduce_fusion
  2239.4 93.6 %all-reduce = (f32[]{:T(128)}, f32[]{:T(128)}) all-reduce(f32[]{:T(128)} %get-tuple-element.6, f32[]{:T(128)} %get-tuple-element.4), channel_id=1, replica_groups=mesh['gx'=8,'gy'=4,'gz'=4] {'gx','gy','gz'}, use_global_device_ids=true, to_apply=%region_15.20 | all-reduce | flops 2 | bytes 16 | tf_op jit(solution)/shard_map/psum | solution.py:120
  (138 shorter events, 7.1 us)
Async XLA Ops:
  7.2 23.3 copy-start
  7.2 650.4 %reduce-scatter.4.cloned.1.call-start = ((), (), s32[]{:S(2)}) async-start(), calls=%async_computation.3 | async-start | bytes 1056768 | tf_op jit(solution)/shard_map/reduce_scatter | solution.py:114
  8.0 141.9 %collective-permute-start.1 = (bf16[16,128]{1,0:T(8,128)(2,1)S(1)}, bf16[16,128]{1,0:T(8,128)(2,1)S(1)}, u32[]{:S(2)}, u32[]{:S(2)}) collective-permute-start(bf16[16,128]{1,0:T(8,128)(2,1)S(1)} %convert_element_type.34), channel_id=1, source_target_pairs={{1,0},{2,1},{3,2},{4,3},{5,4},{6,5},{7,6},{8,7},{9,8},{10,9},{11,1... | collective-permute-start | bytes 12296 | tf_op jit(solution)/shard_map/ppermute | solution.py:20
  17.5 132.4 %collective-permute-start = (bf16[16,128]{1,0:T(8,128)(2,1)S(1)}, bf16[16,128]{1,0:T(8,128)(2,1)S(1)}, u32[]{:S(2)}, u32[]{:S(2)}) collective-permute-start(bf16[16,128]{1,0:T(8,128)(2,1)S(1)} %convert_element_type.34), channel_id=1, source_target_pairs={{0,1},{1,2},{2,3},{3,4},{4,5},{5,6},{6,7},{7,8},{8,9},{9,10},{10,1... | collective-permute-start | bytes 12296 | tf_op jit(solution)/shard_map/ppermute | solution.py:19
  22.3 8.1 copy-start.32
  30.4 16.9 copy-start.31
  30.4 791.3 %copy-start.24 = (pred[512]{0:T(512)(128)(4,1)}, pred[512]{0:T(512)(128)(4,1)S(1)}, u32[]{:S(2)}) copy-start(pred[512]{0:T(512)(128)(4,1)S(1)} %get-tuple-element.26) | copy-start | bytes 1540
  30.4 725.1 %copy-start.19 = (s32[1024]{0:T(1024)}, s32[1024]{0:T(1024)S(1)}, u32[]{:S(2)}) copy-start(s32[1024]{0:T(1024)S(1)} %pad_clamp_fusion) | copy-start | bytes 12292
  31.7 18.9 copy-start.33
  47.2 9.5 copy-start.34
  50.5 1397.3 %reduce-scatter.6.cloned.1.call-start = ((), (), s32[]{:S(2)}) async-start(), calls=%async_computation.4 | async-start | bytes 1056768 | tf_op jit(solution)/shard_map/reduce_scatter | solution.py:114
  50.6 23.2 copy-start.30
  50.6 608.3 %copy-start.13 = (s32[192]{0:T(256)}, s32[192]{0:T(256)S(1)}, u32[]{:S(2)}) copy-start(s32[192]{0:T(256)S(1)} %get-tuple-element.25) | copy-start | bytes 2308
  50.6 763.6 %copy-start.23 = (s32[1024]{0:T(1024)}, s32[1024]{0:T(1024)S(1)}, u32[]{:S(2)}) copy-start(s32[1024]{0:T(1024)S(1)} %pad_clamp_fusion.2) | copy-start | bytes 12292
  52.1 606.8 %copy-start.10 = (f32[192]{0:T(256)}, f32[192]{0:T(256)S(1)}, u32[]{:S(2)}) copy-start(f32[192]{0:T(256)S(1)} %compare_convert_fusion) | copy-start | bytes 2308
  56.8 77.4 %copy-start.16 = (s32[192]{0:T(256)}, s32[192]{0:T(256)S(1)}, u32[]{:S(2)}) copy-start(s32[192]{0:T(256)S(1)} %get-tuple-element.23) | copy-start | bytes 2308
  56.8 93.9 %copy-start.27 = (pred[192]{0:T(512)(128)(4,1)}, pred[192]{0:T(512)(128)(4,1)S(1)}, u32[]{:S(2)}) copy-start(pred[192]{0:T(512)(128)(4,1)S(1)} %get-tuple-element.22) | copy-start | bytes 580
  57.1 601.8 %collective-permute-start.3 = (f32[16,128]{1,0:T(8,128)S(1)}, f32[16,128]{1,0:T(8,128)S(1)}, u32[]{:S(2)}, u32[]{:S(2)}) collective-permute-start(f32[16,128]{1,0:T(8,128)S(1)} %get-tuple-element.33), channel_id=1, source_target_pairs={{1,0},{2,1},{3,2},{4,3},{5,4},{6,5},{7,6},{8,7},{9,8},{10,9},{11,1... | collective-permute-start | bytes 24584 | tf_op jit(solution)/shard_map/ppermute | solution.py:20
  64.1 594.8 %collective-permute-start.2 = (f32[16,128]{1,0:T(8,128)S(1)}, f32[16,128]{1,0:T(8,128)S(1)}, u32[]{:S(2)}, u32[]{:S(2)}) collective-permute-start(f32[16,128]{1,0:T(8,128)S(1)} %get-tuple-element.32), channel_id=1, source_target_pairs={{0,1},{1,2},{2,3},{3,4},{4,5},{5,6},{6,7},{7,8},{8,9},{9,10},{10,1... | collective-permute-start | bytes 24584 | tf_op jit(solution)/shard_map/ppermute | solution.py:19
  133.1 1.2 copy-start.26
  133.1 1.2 copy-start.21
  134.3 524.6 %copy-start.1 = (f32[16,128]{1,0:T(8,128)S(1)}, f32[16,128]{1,0:T(8,128)}, u32[]{:S(2)}) copy-start(f32[16,128]{1,0:T(8,128)} %param.19) | copy-start | bytes 24580
  134.4 524.6 %copy-start.6 = (f32[16,128]{1,0:T(8,128)S(1)}, f32[16,128]{1,0:T(8,128)}, u32[]{:S(2)}) copy-start(f32[16,128]{1,0:T(8,128)} %param.20) | copy-start | bytes 24580
  149.8 605.8 %copy-start.22 = (s32[1024]{0:T(1024)}, s32[1024]{0:T(1024)S(1)}, u32[]{:S(2)}) copy-start(s32[1024]{0:T(1024)S(1)} %pad_clamp_fusion.3) | copy-start | bytes 12292
  815.6 54.7 %collective-permute-start.5 = (bf16[16,128]{1,0:T(8,128)(2,1)S(1)}, bf16[16,128]{1,0:T(8,128)(2,1)}, u32[]{:S(2)}, u32[]{:S(2)}) collective-permute-start(bf16[16,128]{1,0:T(8,128)(2,1)S(1)} %get-tuple-element.20), channel_id=1, source_target_pairs={{1,0},{2,1},{3,2},{4,3},{5,4},{6,5},{7,6},{8,7},{9,8},{10,9},{11,1... | collective-permute-start | bytes 12296 | tf_op jit(solution)/shard_map/ppermute | solution.py:20
  819.8 50.5 %collective-permute-start.4 = (bf16[16,128]{1,0:T(8,128)(2,1)S(1)}, bf16[16,128]{1,0:T(8,128)(2,1)}, u32[]{:S(2)}, u32[]{:S(2)}) collective-permute-start(bf16[16,128]{1,0:T(8,128)(2,1)S(1)} %get-tuple-element.20), channel_id=1, source_target_pairs={{0,1},{1,2},{2,3},{3,4},{4,5},{5,6},{6,7},{7,8},{8,9},{9,10},{10,1... | collective-permute-start | bytes 12296 | tf_op jit(solution)/shard_map/ppermute | solution.py:19
  840.5 18.7 slice-start
  840.5 1396.5 %reduce-scatter.8.cloned.1.call-start = ((), (), s32[]{:S(2)}) async-start(), calls=%async_computation.5 | async-start | bytes 1056768 | tf_op jit(solution)/shard_map/reduce_scatter | solution.py:114
  842.1 16.4 copy-start.3
  842.9 16.3 slice-start.1
  842.9 18.1 copy-start.11
  842.9 18.1 copy-start.17
  842.9 29.0 %copy-start.28 = (pred[192]{0:T(512)(128)(4,1)S(1)}, pred[192]{0:T(512)(128)(4,1)}, u32[]{:S(2)}) copy-start(pred[192]{0:T(512)(128)(4,1)} %copy-done.27) | copy-start | bytes 580
  859.2 589.9 %copy-start.4 = (f32[16,128]{1,0:T(8,128)S(1)}, f32[16,128]{1,0:T(8,128)}, u32[]{:S(2)}) copy-start(f32[16,128]{1,0:T(8,128)} %get-tuple-element.21) | copy-start | bytes 24580
  859.3 589.9 %copy-start.7 = (f32[16,128]{1,0:T(8,128)S(1)}, f32[16,128]{1,0:T(8,128)}, u32[]{:S(2)}) copy-start(f32[16,128]{1,0:T(8,128)} %param.20) | copy-start | bytes 24580
  859.3 589.8 %copy-start.14 = (s32[192]{0:T(256)S(1)}, s32[192]{0:T(256)}, u32[]{:S(2)}) copy-start(s32[192]{0:T(256)} %copy-done.13) | copy-start | bytes 2308
  859.3 686.7 %copy-start.20 = (s32[1024]{0:T(1024)S(1)}, s32[1024]{0:T(1024)}, u32[]{:S(2)}) copy-start(s32[1024]{0:T(1024)} %copy-done.19) | copy-start | bytes 12292
  861.0 751.1 %copy-start.25 = (pred[512]{0:T(512)(128)(4,1)S(1)}, pred[512]{0:T(512)(128)(4,1)}, u32[]{:S(2)}) copy-start(pred[512]{0:T(512)(128)(4,1)} %copy-done.24) | copy-start | bytes 1540
  861.4 587.7 %collective-permute-start.7 = (f32[16,128]{1,0:T(8,128)S(1)}, f32[16,128]{1,0:T(8,128)S(1)}, u32[]{:S(2)}, u32[]{:S(2)}) collective-permute-start(f32[16,128]{1,0:T(8,128)S(1)} %get-tuple-element.31), channel_id=1, source_target_pairs={{1,0},{2,1},{3,2},{4,3},{5,4},{6,5},{7,6},{8,7},{9,8},{10,9},{11,1... | collective-permute-start | bytes 24584 | tf_op jit(solution)/shard_map/ppermute | solution.py:20
  868.3 580.7 %collective-permute-start.6 = (f32[16,128]{1,0:T(8,128)S(1)}, f32[16,128]{1,0:T(8,128)S(1)}, u32[]{:S(2)}, u32[]{:S(2)}) collective-permute-start(f32[16,128]{1,0:T(8,128)S(1)} %get-tuple-element.30), channel_id=1, source_target_pairs={{0,1},{1,2},{2,3},{3,4},{4,5},{5,6},{6,7},{7,8},{8,9},{9,10},{10,1... | collective-permute-start | bytes 24584 | tf_op jit(solution)/shard_map/ppermute | solution.py:19
  1605.8 55.0 %collective-permute-start.9 = (bf16[16,128]{1,0:T(8,128)(2,1)S(1)}, bf16[16,128]{1,0:T(8,128)(2,1)}, u32[]{:S(2)}, u32[]{:S(2)}) collective-permute-start(bf16[16,128]{1,0:T(8,128)(2,1)S(1)} %get-tuple-element.18), channel_id=1, source_target_pairs={{1,0},{2,1},{3,2},{4,3},{5,4},{6,5},{7,6},{8,7},{9,8},{10,9},{11,1... | collective-permute-start | bytes 12296 | tf_op jit(solution)/shard_map/ppermute | solution.py:20
  1610.0 50.9 %collective-permute-start.8 = (bf16[16,128]{1,0:T(8,128)(2,1)S(1)}, bf16[16,128]{1,0:T(8,128)(2,1)}, u32[]{:S(2)}, u32[]{:S(2)}) collective-permute-start(bf16[16,128]{1,0:T(8,128)(2,1)S(1)} %get-tuple-element.18), channel_id=1, source_target_pairs={{0,1},{1,2},{2,3},{3,4},{4,5},{5,6},{6,7},{7,8},{8,9},{9,10},{10,1... | collective-permute-start | bytes 12296 | tf_op jit(solution)/shard_map/ppermute | solution.py:19
  1631.3 18.5 slice-start.2
  1632.6 16.4 copy-start.2
  1633.4 16.3 slice-start.3
  1633.5 18.1 copy-start.12
  1633.5 18.1 copy-start.18
  1633.5 29.0 %copy-start.29 = (pred[192]{0:T(512)(128)(4,1)S(1)}, pred[192]{0:T(512)(128)(4,1)}, u32[]{:S(2)}) copy-start(pred[192]{0:T(512)(128)(4,1)} %copy-done.27) | copy-start | bytes 580
  1649.8 588.6 %copy-start.8 = (f32[16,128]{1,0:T(8,128)S(1)}, f32[16,128]{1,0:T(8,128)}, u32[]{:S(2)}) copy-start(f32[16,128]{1,0:T(8,128)} %param.20) | copy-start | bytes 24580
  1649.8 588.6 %copy-start.9 = (f32[16,128]{1,0:T(8,128)S(1)}, f32[16,128]{1,0:T(8,128)}, u32[]{:S(2)}) copy-start(f32[16,128]{1,0:T(8,128)} %get-tuple-element.19) | copy-start | bytes 24580
  1649.8 588.6 %copy-start.15 = (s32[192]{0:T(256)S(1)}, s32[192]{0:T(256)}, u32[]{:S(2)}) copy-start(s32[192]{0:T(256)} %copy-done.13) | copy-start | bytes 2308
  1649.8 684.4 %copy-start.5 = (f32[16,128]{1,0:T(8,128)S(1)}, f32[16,128]{1,0:T(8,128)}, u32[]{:S(2)}) copy-start(f32[16,128]{1,0:T(8,128)} %get-tuple-element.21) | copy-start | bytes 24580
  1651.9 586.4 %collective-permute-start.11 = (f32[16,128]{1,0:T(8,128)S(1)}, f32[16,128]{1,0:T(8,128)S(1)}, u32[]{:S(2)}, u32[]{:S(2)}) collective-permute-start(f32[16,128]{1,0:T(8,128)S(1)} %get-tuple-element.29), channel_id=1, source_target_pairs={{1,0},{2,1},{3,2},{4,3},{5,4},{6,5},{7,6},{8,7},{9,8},{10,9},{11,1... | collective-permute-start | bytes 24584 | tf_op jit(solution)/shard_map/ppermute | solution.py:20
  1658.9 579.5 %collective-permute-start.10 = (f32[16,128]{1,0:T(8,128)S(1)}, f32[16,128]{1,0:T(8,128)S(1)}, u32[]{:S(2)}, u32[]{:S(2)}) collective-permute-start(f32[16,128]{1,0:T(8,128)S(1)} %get-tuple-element.28), channel_id=1, source_target_pairs={{0,1},{1,2},{2,3},{3,4},{4,5},{5,6},{6,7},{7,8},{8,9},{9,10},{10,1... | collective-permute-start | bytes 24584 | tf_op jit(solution)/shard_map/ppermute | solution.py:19
Sparse Core Ops, SparseCore 0:
  50.6 606.9 reduce-scatter.3
  840.7 607.0 reduce-scatter.5
  1631.4 605.6 reduce-scatter.7
where the time goes:
time: 2350 us; the launch traced here: 2340 us
  waiting for transfers between devices  1640 us (70%)
  blocking collectives  455 us (19%)
  matrix products  127 us (5%)
  starting transfers between devices  50.9 us (2%)
  local copies, waits for them, and re-layouts  30.1 us (1%)
    reduce_scatter x3, waiting for transfers between devices, on_device(): lax.psum_scatter(spread, ('gx', 'gy', 'gz'), scatter_dimension=0, tiled=T...  1640 us
    psum x3, blocking collectives, on_device(): lax.psum((jnp.sum(residual * image), jnp.sum(image * image)), ('gx', 'gy'...  281 us
    all_gather x3, blocking collectives, on_device(): lax.all_gather(own_coeffs, ('gx', 'gy', 'gz'), axis=0, tiled=True)  174 us
  transfers between devices with their start and end apart: 15, of which 3 were waited for; matrix products, arithmetic and copies ran while one was open for 7% of the time, Pallas kernels for 0%

commit v1 on v0

v1 whole, which is shorter than its diff:
```python
import functools

import jax
import jax.numpy as jnp
from jax import lax
from jax.experimental import pallas as pl
from jax.experimental.pallas import tpu as pltpu
from jax.sharding import PartitionSpec as P

ITERS = 3
AXES = ("gx", "gy", "gz")
N = 128
CL = 16
M = 128
R = 32
NEAR = 192
FAR = 512
ROWS = 8
EPS = 1e-6
F32, BF16 = jnp.float32, jnp.bfloat16
LOGICAL = pl.DeviceIdType.LOGICAL


def iota(shape, dim):
    return lax.broadcasted_iota(jnp.int32, shape, dim)


def ones_where(cond):
    return jnp.where(cond, 1.0, 0.0).astype(BF16)


def dot(a, b):
    return jnp.dot(a, b, preferred_element_type=F32)


def dot_t(a, b):
    return lax.dot_general(a, b, (((1,), (1,)), ((), ())), preferred_element_type=F32)


def split(x):
    hi = x.astype(BF16)
    return hi, (x - hi.astype(F32)).astype(BF16)


def kernel(
    rs_ref, diag_ref, near_hbm, nrow_ref, ncol_ref, ncount_ref, basis_ref, coup_hbm, frow_ref, fcol_ref, frank_ref,
    sol_ref, res_ref,
    near, coup, big, t8, e2, fold, hrow, hrow_t, gmask, jmask, hnr, hnc, hnr_t, hnc_t, meta,
    gath, grow, backs, fwds, c4s, send, recv, win, spout, spin, last_out, last_in,
    dma_sem, ssem, rsem, wsem_s, wsem_r, psem_s, psem_r, lsem_s, lsem_r,
):
    me = lax.axis_index(AXES)
    nxt, prv = lax.rem(me + 1, N), lax.rem(me + N - 1, N)
    load_coup = pltpu.make_async_copy(coup_hbm, coup, dma_sem.at[0])
    load_near = pltpu.make_async_copy(near_hbm, near, dma_sem.at[1])
    load_coup.start()
    load_near.start()

    barrier = pltpu.get_barrier_semaphore()

    def greet(o, carry):
        pl.semaphore_signal(barrier, inc=1, device_id=lax.rem(me + o, N), device_id_type=LOGICAL)
        return carry

    lax.fori_loop(1, N, greet, 0)

    frow = frow_ref[...] - me * CL
    fcol = fcol_ref[...]
    owner = fcol // CL
    local = fcol - owner * CL
    rank = frank_ref[...]
    owner_f = owner.astype(F32)
    codes = jnp.concatenate(
        [frow.astype(F32), owner_f, local.astype(F32), rank.astype(F32), jnp.zeros((4, FAR), F32)], axis=0
    )
    codes_t = jnp.transpose(codes)
    frow_c = codes_t[:, 0:1].astype(jnp.int32)
    owner_c = codes_t[:, 1:2].astype(jnp.int32)
    local_c = codes_t[:, 2:3].astype(jnp.int32)
    rank_c = codes_t[:, 3:4].astype(jnp.int32)
    same = jnp.where((owner_c == owner) & (iota((FAR, FAR), 0) < iota((FAR, FAR), 1)), 1.0, 0.0)
    place_f = jnp.sum(same, axis=0, keepdims=True)
    place = place_f.astype(jnp.int32)
    place_c = jnp.transpose(jnp.broadcast_to(place_f, (8, FAR)))[:, 0:1].astype(jnp.int32)

    lane = iota((1, M), 1)
    gmask[...] = ones_where(lane // R == local_c % 4)
    jmask[...] = jnp.where(lane // R == place_c % 4, 1.0, 0.0)
    hrow[...] = ones_where(iota((1, CL), 1) == frow_c)
    hrow_t[...] = ones_where(iota((CL, 1), 0) == frow)
    code_g = owner_c * ROWS + local_c // 4
    big[pl.ds(0, FAR), :] = ones_where(iota((1, N * ROWS), 1) == code_g)
    code_s = owner * ROWS + 4 + place // 4
    t8[...] = ones_where(iota((N * ROWS, 1), 0) == code_s)
    e2[...] = ones_where(iota((M, R * R), 0) % R == iota((M, R * R), 1) // R)
    fold[...] = ones_where(iota((2 * M, M), 0) % R == iota((2 * M, M), 1) % R)
    code_m = owner * ROWS + 7
    t7 = ones_where(iota((N * ROWS, 1), 0) == code_m)
    meta[...] = dot(t7, jnp.where(lane == place_c, local_c.astype(F32), 0.0).astype(BF16))
    big[pl.ds(FAR + 64, 16), :] = ones_where(
        (iota((16, N * ROWS), 0) == 0) & (iota((16, N * ROWS), 1) % ROWS == 6)
    )
    count = ncount_ref[0, 0]
    live = iota((1, NEAR), 1) < count
    nrow = nrow_ref[...] - me * CL
    ncol = ncol_ref[...] - me * CL + CL
    hnr_t[...] = ones_where((iota((CL, 1), 0) == nrow) & live)
    hnc_t[...] = ones_where((iota((3 * CL, 1), 0) == ncol) & live)
    ncodes = jnp.concatenate([nrow.astype(F32), ncol.astype(F32), jnp.zeros((6, NEAR), F32)], axis=0)
    ncodes_t = jnp.transpose(ncodes)
    hnr[...] = ones_where(iota((1, CL), 1) == ncodes_t[:, 0:1].astype(jnp.int32))
    hnc[...] = ones_where(iota((1, 3 * CL), 1) == ncodes_t[:, 1:2].astype(jnp.int32))

    load_coup.wait()
    ab = iota((1, R * R), 1)
    top = jnp.maximum(ab // R, ab % R)
    coup[...] = jnp.where(top < rank_c, coup[...].astype(F32), 0.0).astype(BF16)

    own = iota((CL, CL * R), 1) // R == iota((CL, CL * R), 0)
    rows_of = ones_where(iota((ROWS, CL), 1) // 4 == iota((ROWS, CL), 0))
    even = iota((NEAR, 1), 0) % 2 == 0
    pair_of_row = iota((16, 1), 0) // 2
    odd_row = iota((16, 1), 0) % 2 == 1

    field = rs_ref[...]
    residual = field
    solution = jnp.zeros_like(field)
    sums_tile = jnp.zeros((ROWS, M), F32)
    sub8 = iota((ROWS, M), 0)
    lane8 = iota((ROWS, M), 1)
    image = field

    def to_rows(rw, ww):
        tile = jnp.zeros((ROWS, M), F32)
        for i, value in enumerate((rw, ww)):
            rest = jnp.full((ROWS, M), value, F32)
            for part in range(3):
                piece = rest.astype(BF16).astype(F32)
                rest = rest - piece
                tile = tile + jnp.where((sub8 == 6) & (lane8 == 3 * i + part), piece, 0.0)
        return tile

    for t in range(ITERS):
        low = field.astype(BF16)
        win[t, 1] = low
        if t == 0:
            pl.semaphore_wait(barrier, N - 1)
        to_next = pltpu.make_async_remote_copy(
            win.at[t, 1], win.at[t, 0], wsem_s.at[t, 0], wsem_r.at[t, 0], device_id=nxt, device_id_type=LOGICAL
        )
        to_prev = pltpu.make_async_remote_copy(
            win.at[t, 1], win.at[t, 2], wsem_s.at[t, 1], wsem_r.at[t, 1], device_id=prv, device_id_type=LOGICAL
        )
        to_next.start()
        to_prev.start()

        raw = jnp.where(own, dot_t(low, basis_ref[...]), 0.0)
        coeffs = (raw[:, 0:M] + raw[:, M : 2 * M] + raw[:, 2 * M : 3 * M] + raw[:, 3 * M : 4 * M]).astype(BF16)
        cexp = dot(coeffs, e2[...]).astype(BF16)
        for i in range(8):
            part = pl.ds(i * 64, 64)
            wide = dot(hrow[part, :], cexp)
            prod = coup[part, :].astype(F32) * wide
            acc = prod[:, 0:M]
            for j in range(1, 8):
                acc = acc + prod[:, j * M : (j + 1) * M]
            hi, lo = split(acc)
            summed = dot(jnp.concatenate([hi, lo], axis=1), fold[...])
            c4s[part, :] = (summed * jmask[part, :]).astype(BF16)
        tile = dot(rows_of, coeffs) + sums_tile
        message = dot(t8[...], c4s[...])
        if t == 0:
            message = message + meta[...]
        send[t] = (message.reshape(N, ROWS, M) + tile[None]).astype(BF16)
        recv[t, me] = send[t, me]

        grow_t = dot(hnr[...], low)
        zero = jnp.zeros_like(grow_t)
        grow[...] = jnp.concatenate([jnp.where(even, grow_t, zero), jnp.where(even, zero, grow_t)], axis=1).astype(BF16)

        def far_copy(o, t=t):
            there = lax.rem(me + o, N)
            return pltpu.make_async_remote_copy(
                send.at[t, there], recv.at[t, me], ssem.at[t], rsem.at[t], device_id=there, device_id_type=LOGICAL
            )

        if t == 0:
            load_near.wait()

        for o in range(1, 8):
            far_copy(o).start()

        def near_back(i, carry, far_copy=far_copy):
            for u in range(10):
                far_copy(8 + i * 10 + u).start()
            part = pl.ds(pl.multiple_of(i * 16, 16), 16)
            lhs = grow[part, :]
            out = jnp.zeros((16, M), F32)
            for j in range(8):
                block = near[pl.ds(pl.multiple_of(i * 16 + 2 * j, 2), 2)].reshape(2 * M, M)
                out = jnp.where(pair_of_row == j, dot(lhs, block), out)
            backs[part, :] = out
            return carry

        lax.fori_loop(0, 12, near_back, 0)
        hi, lo = split(backs[...])
        spilled = dot(hnc_t[...], hi) + dot(hnc_t[...], lo)
        spout[t, 0] = spilled[0:CL]
        spout[t, 1] = spilled[2 * CL : 3 * CL]
        spill_prev = pltpu.make_async_remote_copy(
            spout.at[t, 0], spin.at[t, 1], psem_s.at[t, 0], psem_r.at[t, 1], device_id=prv, device_id_type=LOGICAL
        )
        spill_next = pltpu.make_async_remote_copy(
            spout.at[t, 1], spin.at[t, 0], psem_s.at[t, 1], psem_r.at[t, 0], device_id=nxt, device_id_type=LOGICAL
        )
        spill_prev.start()
        spill_next.start()

        to_next.wait_recv()
        to_prev.wait_recv()
        gath[...] = dot(hnc[...], win[t].reshape(3 * CL, M)).astype(BF16)

        def near_forward(i, carry):
            part = pl.ds(pl.multiple_of(i * 16, 16), 16)
            lhs = gath[part, :]
            out = jnp.zeros((16, M), F32)
            for j in range(8):
                block = near[pl.ds(pl.multiple_of(i * 16 + 2 * j, 2), 2)].reshape(2 * M, M)
                got = dot_t(lhs, block)
                got = jnp.where(odd_row, got[:, M:], got[:, :M])
                out = jnp.where(pair_of_row == j, got, out)
            fwds[part, :] = out
            return carry

        lax.fori_loop(0, 12, near_forward, 0)
        hi, lo = split(fwds[...])
        product = diag_ref[...] * field + spilled[CL : 2 * CL] + dot(hnr_t[...], hi) + dot(hnr_t[...], lo)

        everyone = recv.at[t, pl.ds(0, N - 1)]
        pltpu.make_async_copy(everyone, everyone, rsem.at[t]).wait()
        arrived = recv[t].reshape(N * ROWS, M)
        if t == 0:
            pick = ones_where(iota((16, M), 1) == iota((16, M), 0))
            numbers = dot_t(pick, arrived)
            col = iota((1, N * ROWS), 1) % ROWS
            first = jnp.concatenate([numbers[:, 3:], numbers[:, :3]], axis=1)
            second = jnp.concatenate([numbers[:, 2:], numbers[:, :2]], axis=1)
            pieces = []
            for q in range(4):
                number = jnp.where(col == 4, first[q : q + 1], jnp.where(col == 5, second[4 + q : 5 + q], -1.0))
                pieces.append(ones_where(iota((CL, 1), 0).astype(F32) == number))
            big[pl.ds(FAR, 64), :] = jnp.concatenate(pieces, axis=0)
        got = dot(big[...], arrived)
        totals = got[FAR + 64 : FAR + 65, :]
        c4s[...] = dot(got[0:FAR].astype(BF16) * gmask[...], fold[0:M, :]).astype(BF16)
        z = jnp.zeros((CL, R * R), F32)
        for i in range(4):
            part = pl.ds(i * 128, 128)
            c4 = c4s[part, :].astype(F32)
            prods = coup[part, :].astype(F32) * jnp.concatenate([c4] * 8, axis=1)
            hi, lo = split(prods)
            z = z + dot(hrow_t[:, i * 128 : (i + 1) * 128], hi) + dot(hrow_t[:, i * 128 : (i + 1) * 128], lo)
        hi, lo = split(z)
        farsum = dot_t(hi, e2[...]) + dot_t(lo, e2[...])
        slots = jnp.zeros((CL, M), F32)
        for q in range(4):
            slots = slots + jnp.where(lane // R == q, got[FAR + 16 * q : FAR + 16 * (q + 1), :], 0.0)
        hi, lo = split(slots)
        farsum = farsum + dot(jnp.concatenate([hi, lo], axis=1), fold[...])
        diag_far = jnp.where(own, jnp.concatenate([farsum] * 4, axis=1), 0.0).astype(BF16)
        product = product + dot(diag_far, basis_ref[...])

        spill_prev.wait_recv()
        spill_next.wait_recv()
        product = product + spin[t, 0] + spin[t, 1]

        if t == 0:
            image = product
        else:
            rw = totals[:, 0:1] + totals[:, 1:2] + totals[:, 2:3]
            ww = totals[:, 3:4] + totals[:, 4:5] + totals[:, 5:6]
            step = rw / (ww + EPS)
            solution = solution + step * residual
            residual = residual - step * image
            image = image - step * product
        field = image
        if t + 1 < ITERS:
            sums_tile = to_rows(jnp.sum(residual * image), jnp.sum(image * image))

    rw, ww = jnp.sum(residual * image), jnp.sum(image * image)
    last_out[...] = jnp.where(lane == 0, rw, jnp.where(lane == 1, ww, 0.0))
    last_in[me] = last_out[...]

    def last_copy(o, carry):
        pltpu.make_async_remote_copy(
            last_out, last_in.at[me], lsem_s, lsem_r, device_id=lax.rem(me + o, N), device_id_type=LOGICAL
        ).start()
        return carry

    lax.fori_loop(1, N, last_copy, 0)
    everyone = last_in.at[pl.ds(0, N - 1)]
    pltpu.make_async_copy(everyone, everyone, lsem_r).wait()
    totals = jnp.sum(last_in[...], axis=0)
    step = totals[:, 0:1] / (totals[:, 1:2] + EPS)
    sol_ref[...] = solution + step * residual
    res_ref[...] = residual - step * image

    pltpu.make_async_copy(everyone, everyone, lsem_s).wait()
    for t in range(ITERS):
        sent = send.at[t, pl.ds(0, N - 1)]
        pltpu.make_async_copy(sent, sent, ssem.at[t]).wait()
        for i in range(2):
            pltpu.make_async_copy(win.at[t, 1], win.at[t, 1], wsem_s.at[t, i]).wait()
            pltpu.make_async_copy(spout.at[t, i], spout.at[t, i], psem_s.at[t, i]).wait()


def on_device(rs, diag, near, nrow, ncol, ncount, basis, coup, frow, fcol, frank):
    vmem = pl.BlockSpec(memory_space=pltpu.VMEM)
    smem = pl.BlockSpec(memory_space=pltpu.SMEM)
    hbm = pl.BlockSpec(memory_space=pl.ANY)
    v = pltpu.VMEM
    dma = pltpu.SemaphoreType.DMA
    shape = jax.ShapeDtypeStruct((CL, M), F32)
    return pl.pallas_call(
        kernel,
        out_shape=(shape, shape),
        in_specs=[vmem, vmem, hbm, vmem, vmem, smem, vmem, hbm, vmem, vmem, vmem],
        out_specs=(vmem, vmem),
        scratch_shapes=[
            v((NEAR, M, M), BF16),
            v((FAR, R * R), BF16),
            v((FAR + 80, N * ROWS), BF16),
            v((N * ROWS, FAR), BF16),
            v((M, R * R), BF16),
            v((2 * M, M), BF16),
            v((FAR, CL), BF16),
            v((CL, FAR), BF16),
            v((FAR, M), BF16),
            v((FAR, M), F32),
            v((NEAR, CL), BF16),
            v((NEAR, 3 * CL), BF16),
            v((CL, NEAR), BF16),
            v((3 * CL, NEAR), BF16),
            v((N * ROWS, M), F32),
            v((NEAR, M), BF16),
            v((NEAR, 2 * M), BF16),
            v((NEAR, M), F32),
            v((NEAR, M), F32),
            v((FAR, M), BF16),
            v((ITERS, N, ROWS, M), BF16),
            v((ITERS, N, ROWS, M), BF16),
            v((ITERS, 3, CL, M), BF16),
            v((ITERS, 2, CL, M), F32),
            v((ITERS, 2, CL, M), F32),
            v((1, M), F32),
            v((N, 1, M), F32),
            dma((2,)),
            dma((ITERS,)),
            dma((ITERS,)),
            dma((ITERS, 2)),
            dma((ITERS, 2)),
            dma((ITERS, 2)),
            dma((ITERS, 2)),
            dma,
            dma,
        ],
        compiler_params=pltpu.CompilerParams(
            collective_id=0, has_side_effects=True, vmem_limit_bytes=48 << 20
        ),
    )(
        rs,
        diag,
        near,
        nrow.reshape(1, NEAR),
        ncol.reshape(1, NEAR),
        ncount.reshape(1, 1),
        basis.reshape(CL * R, M),
        coup,
        frow.reshape(1, FAR),
        fcol.reshape(1, FAR),
        frank.reshape(1, FAR),
    )


def solution(mesh):
    flat = P(AXES)
    two = P(AXES, None)
    three = P(AXES, None, None)
    return jax.shard_map(
        on_device,
        mesh=mesh,
        in_specs=(two, two, three, flat, flat, flat, three, two, flat, flat, flat),
        out_specs=(two, two),
        check_vma=False,
    )
```

time: 2350 us -> 64 us (0.03)
  waiting for transfers between devices: 1640 us -> 0 us
  blocking collectives: 455 us -> 0 us
  matrix products: 127 us -> 0 us
  Pallas kernels: 0 us -> 54.2 us
  starting transfers between devices: 50.9 us -> 0 us
    reduce_scatter x3 -> x0, waiting for transfers between devices: 1640 us -> none  [on_device(): lax.psum_scatter(spread, ('gx', 'gy', 'gz'), scatter_dimension=0, tiled=T...]
    psum x3 -> x0, blocking collectives: 281 us -> none  [on_device(): lax.psum((jnp.sum(residual * image), jnp.sum(image * image)), ('gx', 'gy'...]
    all_gather x3 -> x0, blocking collectives: 174 us -> none  [on_device(): lax.all_gather(own_coeffs, ('gx', 'gy', 'gz'), axis=0, tiled=True)]
    dot_general x27 -> x0, matrix products: 127 us -> none  [the longest x3 46.5 us: on_device(): jnp.einsum('kab,kb->ka', coupled, jnp.take(all_coeffs, far_cols, axis=0),...]
    pallas_call x0 -> x1, Pallas kernels: none -> 54.2 us  [on_device(): pl.pallas_call(kernel, out_shape=(shape, shape), in_specs=[vmem, vmem, hb...]
    ppermute x12 -> x0, starting transfers between devices: 50.6 us -> none  [the longest x6 38.7 us: extended(): after = lax.ppermute(initial, axis, down)]
  transfers between devices with their start and end apart: 15 -> 0, of which waited for: 3 -> 0; matrix products, arithmetic and copies ran while one was open for 7% -> 0% of each run, Pallas kernels for 0% -> 0%
where the time goes in v1:
time: 64 us; the launch traced here: 63.6 us
  Pallas kernels  54.2 us (85%)
  local copies, waits for them, and re-layouts  8.11 us (13%)
  between operations  1.3 us (2%)
    pallas_call x1, Pallas kernels, on_device(): pl.pallas_call(kernel, out_shape=(shape, shape), in_specs=[vmem, vmem, hb...  54.2 us
    unnamed x20, local copies, waits for them, and re-layouts  8.11 us

profile of v1, /device:TPU:1, one launch (start us, length us, event | category | flops | bytes accessed | tf_op | source)
XLA Modules:
  0.0 63.6 jit_solution(16935847820021306035)
XLA Ops:
  1.3 0.0 copy-start
  1.3 1.2 %copy-done = bf16[512,1024]{1,0:T(8,128)(2,1)S(1)} copy-done((bf16[512,1024]{1,0:T(8,128)(2,1)S(1)}, bf16[512,1024]{1,0:T(8,128)(2,1)}, u32[]{:S(2)}) %copy-start) | copy-done | bytes 1048600
  2.5 0.0 copy-start.1
  2.5 0.9 %copy-done.1 = bf16[16,32,128]{2,1,0:T(8,128)(2,1)S(1)} copy-done((bf16[16,32,128]{2,1,0:T(8,128)(2,1)S(1)}, bf16[16,32,128]{2,1,0:T(8,128)(2,1)}, u32[]{:S(2)}) %copy-start.1) | copy-done | bytes 131096
  3.4 0.0 copy-start.2
  3.4 0.7 %copy-done.2 = f32[16,128]{1,0:T(8,128)S(1)} copy-done((f32[16,128]{1,0:T(8,128)S(1)}, f32[16,128]{1,0:T(8,128)}, u32[]{:S(2)}) %copy-start.2) | copy-done | bytes 8216
  4.1 0.0 copy-start.3
  4.1 0.7 %copy-done.3 = f32[16,128]{1,0:T(8,128)S(1)} copy-done((f32[16,128]{1,0:T(8,128)S(1)}, f32[16,128]{1,0:T(8,128)}, u32[]{:S(2)}) %copy-start.3) | copy-done | bytes 8216
  4.8 0.0 copy-start.4
  4.8 0.7 %copy-done.4 = s32[512]{0:T(512)S(1)} copy-done((s32[512]{0:T(512)S(1)}, s32[512]{0:T(512)}, u32[]{:S(2)}) %copy-start.4) | copy-done | bytes 2072
  5.5 0.0 copy-start.5
  5.5 0.7 %copy-done.5 = s32[512]{0:T(512)S(1)} copy-done((s32[512]{0:T(512)S(1)}, s32[512]{0:T(512)}, u32[]{:S(2)}) %copy-start.5) | copy-done | bytes 2072
  6.2 0.0 copy-start.6
  6.2 0.7 %copy-done.6 = s32[512]{0:T(512)S(1)} copy-done((s32[512]{0:T(512)S(1)}, s32[512]{0:T(512)}, u32[]{:S(2)}) %copy-start.6) | copy-done | bytes 2072
  6.9 0.0 copy-start.7
  6.9 0.7 %copy-done.7 = s32[192]{0:T(256)S(1)} copy-done((s32[192]{0:T(256)S(1)}, s32[192]{0:T(256)}, u32[]{:S(2)}) %copy-start.7) | copy-done | bytes 792
  7.5 0.0 copy-start.8
  7.5 0.7 %copy-done.8 = s32[192]{0:T(256)S(1)} copy-done((s32[192]{0:T(256)S(1)}, s32[192]{0:T(256)}, u32[]{:S(2)}) %copy-start.8) | copy-done | bytes 792
  8.2 54.2 %shard_map.122 = (f32[16,128]{1,0:T(8,128)S(1)}, f32[16,128]{1,0:T(8,128)S(1)}) custom-call(f32[16,128]{1,0:T(8,128)S(1)} %copy-done.2, f32[16,128]{1,0:T(8,128)S(1)} %copy-done.3, bf16[192,128,128]{2,1,0:T(8,128)(2,1)} %near_hbm.1, s32[1,192]{1,0:T(1,128)S(1)} %bitcast.12, s32[1,192]{1,0:T(1,128)S(1)} %bitcast.13, s32[1,1]{1,0:T(1,128)} %bitcast.7.ncount_ref, ...), custom_call_target="tpu_custom_call" | custom-call | tf_op jit(solution)/shard_map/pallas_call | solution.py:324
  62.4 0.6 copy.16
  63.0 0.6 copy.17
Async XLA Ops:
  1.3 1.2 %copy-start = (bf16[512,1024]{1,0:T(8,128)(2,1)S(1)}, bf16[512,1024]{1,0:T(8,128)(2,1)}, u32[]{:S(2)}) copy-start(bf16[512,1024]{1,0:T(8,128)(2,1)} %coup_hbm.1) | copy-start | bytes 3145732
  2.5 0.9 %copy-start.1 = (bf16[16,32,128]{2,1,0:T(8,128)(2,1)S(1)}, bf16[16,32,128]{2,1,0:T(8,128)(2,1)}, u32[]{:S(2)}) copy-start(bf16[16,32,128]{2,1,0:T(8,128)(2,1)} %param.17) | copy-start | bytes 393220
  3.4 0.7 %copy-start.2 = (f32[16,128]{1,0:T(8,128)S(1)}, f32[16,128]{1,0:T(8,128)}, u32[]{:S(2)}) copy-start(f32[16,128]{1,0:T(8,128)} %rs_ref.1) | copy-start | bytes 24580
  4.1 0.7 %copy-start.3 = (f32[16,128]{1,0:T(8,128)S(1)}, f32[16,128]{1,0:T(8,128)}, u32[]{:S(2)}) copy-start(f32[16,128]{1,0:T(8,128)} %diag_ref.1) | copy-start | bytes 24580
  4.8 0.7 %copy-start.4 = (s32[512]{0:T(512)S(1)}, s32[512]{0:T(512)}, u32[]{:S(2)}) copy-start(s32[512]{0:T(512)} %param.19) | copy-start | bytes 6148
  5.5 0.7 %copy-start.5 = (s32[512]{0:T(512)S(1)}, s32[512]{0:T(512)}, u32[]{:S(2)}) copy-start(s32[512]{0:T(512)} %param.20) | copy-start | bytes 6148
  6.2 0.7 %copy-start.6 = (s32[512]{0:T(512)S(1)}, s32[512]{0:T(512)}, u32[]{:S(2)}) copy-start(s32[512]{0:T(512)} %param.21) | copy-start | bytes 6148
  6.9 0.7 %copy-start.7 = (s32[192]{0:T(256)S(1)}, s32[192]{0:T(256)}, u32[]{:S(2)}) copy-start(s32[192]{0:T(256)} %param.14) | copy-start | bytes 2308
  7.5 0.7 %copy-start.8 = (s32[192]{0:T(256)S(1)}, s32[192]{0:T(256)}, u32[]{:S(2)}) copy-start(s32[192]{0:T(256)} %param.15) | copy-start | bytes 2308

commit v2 on v1

--- a/solution.py
+++ b/solution.py
@@ -21,6 +21,26 @@
 LOGICAL = pl.DeviceIdType.LOGICAL
 
 
+STEPS = sorted(
+    ((code, core) for code in range(64) for core in range(2) if (code, core) != (0, 0)),
+    key=lambda s: (-bin(s[0]).count("1"), s[0], s[1]),
+)
+GRAY = (0, 1, 3, 2)
+FIRST = 44
+
+
+def partners():
+    gx, gy, gz = lax.axis_index("gx"), lax.axis_index("gy"), lax.axis_index("gz")
+    x, core = gx // 2, gx % 2
+    xs = [((x + step) % 4) * 32 for step in range(4)]
+    cores = [core * 16, (1 - core) * 16]
+    zs = [((gy + step) % 4) * 4 for step in range(4)]
+    ys = [(gz + step) % 4 for step in range(4)]
+    return [
+        xs[GRAY[code // 16]] + cores[other] + zs[GRAY[code // 4 % 4]] + ys[GRAY[code % 4]] for code, other in STEPS
+    ]
+
+
 def iota(shape, dim):
     return lax.broadcasted_iota(jnp.int32, shape, dim)
 
@@ -35,6 +55,15 @@
 
 def dot_t(a, b):
     return lax.dot_general(a, b, (((1,), (1,)), ((), ())), preferred_element_type=F32)
+
+
+def copies(x):
+    x = x + pltpu.roll(x, 2 * R, 1)
+    return x + pltpu.roll(x, R, 1)
+
+
+def whole(x):
+    return jnp.sum(jnp.sum(x, axis=0, keepdims=True), axis=1, keepdims=True)
 
 
 def split(x):
@@ -43,9 +72,10 @@
 
 
 def kernel(
-    rs_ref, diag_ref, near_hbm, nrow_ref, ncol_ref, ncount_ref, basis_ref, coup_hbm, frow_ref, fcol_ref, frank_ref,
-    sol_ref, res_ref,
-    near, coup, big, t8, e2, fold, hrow, hrow_t, gmask, jmask, hnr, hnc, hnr_t, hnc_t, meta,
+    rs_hbm, diag_hbm, near_hbm, nrow_hbm, ncol_hbm, ncount_hbm, basis_hbm, coup_hbm, frow_hbm, fcol_hbm, frank_hbm,
+    out_ref,
+    rs_ref, diag_ref, nrow_ref, ncol_ref, ncount_ref, basis_ref, frow_ref, fcol_ref, frank_ref,
+    near, coup, coup_t, big, t8, e2_t, basis_t, hrow, hrow_t, gmask, jmask, hnr, hnc, hnr_t, hnc_t, meta,
     gath, grow, backs, fwds, c4s, send, recv, win, spout, spin, last_out, last_in,
     dma_sem, ssem, rsem, wsem_s, wsem_r, psem_s, psem_r, lsem_s, lsem_r,
 ):
@@ -53,16 +83,23 @@
     nxt, prv = lax.rem(me + 1, N), lax.rem(me + N - 1, N)
     load_coup = pltpu.make_async_copy(coup_hbm, coup, dma_sem.at[0])
     load_near = pltpu.make_async_copy(near_hbm, near, dma_sem.at[1])
+    pairs = (
+        (frow_hbm, frow_ref), (fcol_hbm, fcol_ref), (frank_hbm, frank_ref), (nrow_hbm, nrow_ref), (ncol_hbm, ncol_ref),
+        (ncount_hbm, ncount_ref), (rs_hbm, rs_ref), (basis_hbm, basis_ref), (diag_hbm, diag_ref),
+    )
+    loads = [pltpu.make_async_copy(a, b, dma_sem.at[2 + i]) for i, (a, b) in enumerate(pairs)]
+    for load in loads:
+        load.start()
     load_coup.start()
     load_near.start()
 
     barrier = pltpu.get_barrier_semaphore()
 
-    def greet(o, carry):
-        pl.semaphore_signal(barrier, inc=1, device_id=lax.rem(me + o, N), device_id_type=LOGICAL)
-        return carry
-
-    lax.fori_loop(1, N, greet, 0)
+    others = partners()
+    for there in others:
+        pl.semaphore_signal(barrier, inc=1, device_id=there, device_id_type=LOGICAL)
+    for load in loads:
+        load.wait()
 
     frow = frow_ref[...] - me * CL
     fcol = fcol_ref[...]
@@ -84,7 +121,7 @@
     place_c = jnp.transpose(jnp.broadcast_to(place_f, (8, FAR)))[:, 0:1].astype(jnp.int32)
 
     lane = iota((1, M), 1)
-    gmask[...] = ones_where(lane // R == local_c % 4)
+    gmask[...] = jnp.where(lane // R == local_c % 4, 1.0, 0.0)
     jmask[...] = jnp.where(lane // R == place_c % 4, 1.0, 0.0)
     hrow[...] = ones_where(iota((1, CL), 1) == frow_c)
     hrow_t[...] = ones_where(iota((CL, 1), 0) == frow)
@@ -92,8 +129,9 @@
     big[pl.ds(0, FAR), :] = ones_where(iota((1, N * ROWS), 1) == code_g)
     code_s = owner * ROWS + 4 + place // 4
     t8[...] = ones_where(iota((N * ROWS, 1), 0) == code_s)
-    e2[...] = ones_where(iota((M, R * R), 0) % R == iota((M, R * R), 1) // R)
-    fold[...] = ones_where(iota((2 * M, M), 0) % R == iota((2 * M, M), 1) % R)
+    e2_t[...] = ones_where(iota((R * R, M), 0) // R == iota((R * R, M), 1) % R)
+    eye = ones_where(iota((M, M), 0) == iota((M, M), 1))
+    basis_t[...] = dot_t(eye, basis_ref[...]).astype(BF16)
     code_m = owner * ROWS + 7
     t7 = ones_where(iota((N * ROWS, 1), 0) == code_m)
     meta[...] = dot(t7, jnp.where(lane == place_c, local_c.astype(F32), 0.0).astype(BF16))
@@ -115,6 +153,10 @@
     ab = iota((1, R * R), 1)
     top = jnp.maximum(ab // R, ab % R)
     coup[...] = jnp.where(top < rank_c, coup[...].astype(F32), 0.0).astype(BF16)
+    flip = ones_where(iota((R * R, 1), 0) == (ab % R) * R + ab // R)
+    for i in range(4):
+        part = pl.ds(i * 128, 128)
+        coup_t[part, :] = dot(coup[part, :], flip).astype(BF16)
 
     own = iota((CL, CL * R), 1) // R == iota((CL, CL * R), 0)
     rows_of = ones_where(iota((ROWS, CL), 1) // 4 == iota((ROWS, CL), 0))
@@ -133,7 +175,7 @@
     def to_rows(rw, ww):
         tile = jnp.zeros((ROWS, M), F32)
         for i, value in enumerate((rw, ww)):
-            rest = jnp.full((ROWS, M), value, F32)
+            rest = jnp.broadcast_to(value, (ROWS, M))
             for part in range(3):
                 piece = rest.astype(BF16).astype(F32)
                 rest = rest - piece
@@ -154,19 +196,18 @@
         to_next.start()
         to_prev.start()
 
-        raw = jnp.where(own, dot_t(low, basis_ref[...]), 0.0)
+        raw = jnp.where(own, dot(low, basis_t[...]), 0.0)
         coeffs = (raw[:, 0:M] + raw[:, M : 2 * M] + raw[:, 2 * M : 3 * M] + raw[:, 3 * M : 4 * M]).astype(BF16)
-        cexp = dot(coeffs, e2[...]).astype(BF16)
-        for i in range(8):
-            part = pl.ds(i * 64, 64)
-            wide = dot(hrow[part, :], cexp)
-            prod = coup[part, :].astype(F32) * wide
-            acc = prod[:, 0:M]
-            for j in range(1, 8):
-                acc = acc + prod[:, j * M : (j + 1) * M]
-            hi, lo = split(acc)
-            summed = dot(jnp.concatenate([hi, lo], axis=1), fold[...])
-            c4s[part, :] = (summed * jmask[part, :]).astype(BF16)
+        wide = dot(hrow[...], copies(coeffs.astype(F32)).astype(BF16)).astype(BF16)
+        if t == 0:
+            for i in range(4):
+                part = pl.ds(i * 128, 128)
+                prods = coup_t[part, :].astype(F32) * jnp.concatenate([wide[i * 128 : (i + 1) * 128].astype(F32)] * 8, axis=1)
+                hi, lo = split(prods)
+                c4s[part, :] = ((dot(hi, e2_t[...]) + dot(lo, e2_t[...])) * jmask[part, :]).astype(BF16)
+        else:
+            prods = coup_t[...] * jnp.concatenate([wide] * 8, axis=1)
+            c4s[...] = (dot(prods, e2_t[...]) * jmask[...]).astype(BF16)
         tile = dot(rows_of, coeffs) + sums_tile
         message = dot(t8[...], c4s[...])
         if t == 0:
@@ -178,31 +219,31 @@
         zero = jnp.zeros_like(grow_t)
         grow[...] = jnp.concatenate([jnp.where(even, grow_t, zero), jnp.where(even, zero, grow_t)], axis=1).astype(BF16)
 
-        def far_copy(o, t=t):
-            there = lax.rem(me + o, N)
+        def far_copy(there, t=t):
             return pltpu.make_async_remote_copy(
                 send.at[t, there], recv.at[t, me], ssem.at[t], rsem.at[t], device_id=there, device_id_type=LOGICAL
             )
 
+        for there in others[:FIRST]:
+            far_copy(there).start()
+
         if t == 0:
             load_near.wait()
 
-        for o in range(1, 8):
-            far_copy(o).start()
-
-        def near_back(i, carry, far_copy=far_copy):
-            for u in range(10):
-                far_copy(8 + i * 10 + u).start()
-            part = pl.ds(pl.multiple_of(i * 16, 16), 16)
+        def near_back(i, carry):
+            for there in others[FIRST + 7 * i : FIRST + 7 * i + 7]:
+                far_copy(there).start()
+            part = pl.ds(i * 16, 16)
             lhs = grow[part, :]
             out = jnp.zeros((16, M), F32)
             for j in range(8):
-                block = near[pl.ds(pl.multiple_of(i * 16 + 2 * j, 2), 2)].reshape(2 * M, M)
+                block = near[pl.ds(i * 16 + 2 * j, 2)].reshape(2 * M, M)
                 out = jnp.where(pair_of_row == j, dot(lhs, block), out)
             backs[part, :] = out
             return carry
 
-        lax.fori_loop(0, 12, near_back, 0)
+        for i in range(12):
+            near_back(i, 0)
         hi, lo = split(backs[...])
         spilled = dot(hnc_t[...], hi) + dot(hnc_t[...], lo)
         spout[t, 0] = spilled[0:CL]
@@ -252,21 +293,24 @@
             big[pl.ds(FAR, 64), :] = jnp.concatenate(pieces, axis=0)
         got = dot(big[...], arrived)
         totals = got[FAR + 64 : FAR + 65, :]
-        c4s[...] = dot(got[0:FAR].astype(BF16) * gmask[...], fold[0:M, :]).astype(BF16)
-        z = jnp.zeros((CL, R * R), F32)
-        for i in range(4):
-            part = pl.ds(i * 128, 128)
-            c4 = c4s[part, :].astype(F32)
-            prods = coup[part, :].astype(F32) * jnp.concatenate([c4] * 8, axis=1)
-            hi, lo = split(prods)
-            z = z + dot(hrow_t[:, i * 128 : (i + 1) * 128], hi) + dot(hrow_t[:, i * 128 : (i + 1) * 128], lo)
+        c4s[...] = copies(got[0:FAR] * gmask[...]).astype(BF16)
+        if t == 0:
+            z = jnp.zeros((CL, R * R), F32)
+            for i in range(4):
+                part = pl.ds(i * 128, 128)
+                c4 = c4s[part, :].astype(F32)
+                hi, lo = split(coup[part, :].astype(F32) * jnp.concatenate([c4] * 8, axis=1))
+                rows = hrow_t[:, i * 128 : (i + 1) * 128]
+                z = z + dot(rows, hi) + dot(rows, lo)
+        else:
+            z = dot(hrow_t[...], coup[...] * jnp.concatenate([c4s[...]] * 8, axis=1))
         hi, lo = split(z)
-        farsum = dot_t(hi, e2[...]) + dot_t(lo, e2[...])
+        farsum = dot(jnp.concatenate([hi, lo], axis=0), e2_t[...])
+        farsum = farsum[0:CL] + farsum[CL:]
         slots = jnp.zeros((CL, M), F32)
         for q in range(4):
             slots = slots + jnp.where(lane // R == q, got[FAR + 16 * q : FAR + 16 * (q + 1), :], 0.0)
-        hi, lo = split(slots)
-        farsum = farsum + dot(jnp.concatenate([hi, lo], axis=1), fold[...])
+        farsum = farsum + copies(slots)
         diag_far = jnp.where(own, jnp.concatenate([farsum] * 4, axis=1), 0.0).astype(BF16)
         product = product + dot(diag_far, basis_ref[...])
 
@@ -285,25 +329,24 @@
             image = image - step * product
         field = image
         if t + 1 < ITERS:
-            sums_tile = to_rows(jnp.sum(residual * image), jnp.sum(image * image))
-
-    rw, ww = jnp.sum(residual * image), jnp.sum(image * image)
+            sums_tile = to_rows(whole(residual * image), whole(image * image))
+
+    rw, ww = whole(residual * image), whole(image * image)
     last_out[...] = jnp.where(lane == 0, rw, jnp.where(lane == 1, ww, 0.0))
     last_in[me] = last_out[...]
 
-    def last_copy(o, carry):
+    for there in others:
         pltpu.make_async_remote_copy(
-            last_out, last_in.at[me], lsem_s, lsem_r, device_id=lax.rem(me + o, N), device_id_type=LOGICAL
+            last_out, last_in.at[me], lsem_s, lsem_r, device_id=there, device_id_type=LOGICAL
         ).start()
-        return carry
-
-    lax.fori_loop(1, N, last_copy, 0)
     everyone = last_in.at[pl.ds(0, N - 1)]
     pltpu.make_async_copy(everyone, everyone, lsem_r).wait()
     totals = jnp.sum(last_in[...], axis=0)
     step = totals[:, 0:1] / (totals[:, 1:2] + EPS)
-    sol_ref[...] = solution + step * residual
-    res_ref[...] = residual - step * image
+    out_ref[0] = solution
+    out_ref[1] = residual
+    out_ref[2] = image
+    out_ref[3] = jnp.broadcast_to(step, (CL, M))
 
     pltpu.make_async_copy(everyone, everyone, lsem_s).wait()
     for t in range(ITERS):
@@ -316,26 +359,35 @@
 
 def on_device(rs, diag, near, nrow, ncol, ncount, basis, coup, frow, fcol, frank):
     vmem = pl.BlockSpec(memory_space=pltpu.VMEM)
-    smem = pl.BlockSpec(memory_space=pltpu.SMEM)
     hbm = pl.BlockSpec(memory_space=pl.ANY)
+    ints = jnp.int32
     v = pltpu.VMEM
     dma = pltpu.SemaphoreType.DMA
-    shape = jax.ShapeDtypeStruct((CL, M), F32)
-    return pl.pallas_call(
+    out = pl.pallas_call(
         kernel,
-        out_shape=(shape, shape),
-        in_specs=[vmem, vmem, hbm, vmem, vmem, smem, vmem, hbm, vmem, vmem, vmem],
-        out_specs=(vmem, vmem),
+        out_shape=jax.ShapeDtypeStruct((4, CL, M), F32),
+        in_specs=[hbm] * 11,
+        out_specs=vmem,
         scratch_shapes=[
+            v((CL, M), F32),
+            v((CL, M), F32),
+            v((1, NEAR), ints),
+            v((1, NEAR), ints),
+            pltpu.SMEM((1, 1), ints),
+            v((CL * R, M), BF16),
+            v((1, FAR), ints),
+            v((1, FAR), ints),
+            v((1, FAR), ints),
             v((NEAR, M, M), BF16),
+            v((FAR, R * R), BF16),
             v((FAR, R * R), BF16),
             v((FAR + 80, N * ROWS), BF16),
             v((N * ROWS, FAR), BF16),
-            v((M, R * R), BF16),
-            v((2 * M, M), BF16),
+            v((R * R, M), BF16),
+            v((M, CL * R), BF16),
             v((FAR, CL), BF16),
             v((CL, FAR), BF16),
-            v((FAR, M), BF16),
+            v((FAR, M), F32),
             v((FAR, M), F32),
             v((NEAR, CL), BF16),
             v((NEAR, 3 * CL), BF16),
@@ -354,7 +406,7 @@
             v((ITERS, 2, CL, M), F32),
             v((1, M), F32),
             v((N, 1, M), F32),
-            dma((2,)),
+            dma((11,)),
             dma((ITERS,)),
             dma((ITERS,)),
             dma((ITERS, 2)),
@@ -365,7 +417,7 @@
             dma,
         ],
         compiler_params=pltpu.CompilerParams(
-            collective_id=0, has_side_effects=True, vmem_limit_bytes=48 << 20
+            collective_id=0, has_side_effects=True, vmem_limit_bytes=60 << 20
         ),
     )(
         rs,
@@ -380,6 +432,7 @@
         fcol.reshape(1, FAR),
         frank.reshape(1, FAR),
     )
+    return out[0] + out[3] * out[1], out[1] - out[3] * out[2]
 
 
 def solution(mesh):

time: 64 us -> 50.5 us (0.79)
  local copies, waits for them, and re-layouts: 8.11 us -> 0 us
  Pallas kernels: 54.2 us -> 47.7 us
  other arithmetic: 0 us -> 1.36 us
    unnamed x20 -> x0, local copies, waits for them, and re-layouts: 8.11 us -> none
    pallas_call x1, Pallas kernels: 54.2 us -> 47.7 us  [on_device(): pl.pallas_call(kernel, out_shape=jax.ShapeDtypeStruct((4, CL, M), F32), i...]
    sub x0 -> x1, other arithmetic: none -> 1.36 us  [on_device(): return (out[0] + out[3] * out[1], out[1] - out[3] * out[2])]
where the time goes in v2:
time: 50.5 us; the launch traced here: 50.3 us
  Pallas kernels  47.7 us (94%)
  other arithmetic  1.36 us (3%)
  between operations  1.29 us (3%)
    pallas_call x1, Pallas kernels, on_device(): pl.pallas_call(kernel, out_shape=jax.ShapeDtypeStruct((4, CL, M), F32), i...  47.7 us
    sub x1, other arithmetic, on_device(): return (out[0] + out[3] * out[1], out[1] - out[3] * out[2])  1.36 us

profile of v2, /device:TPU:1, one launch (start us, length us, event | category | flops | bytes accessed | tf_op | source)
XLA Modules:
  0.0 50.3 jit_solution(15783578217464872510)
XLA Ops:
  1.3 47.7 %shard_map.122 = f32[4,16,128]{2,1,0:T(8,128)} custom-call(f32[16,128]{1,0:T(8,128)} %rs_hbm.1, f32[16,128]{1,0:T(8,128)} %diag_hbm.1, bf16[192,128,128]{2,1,0:T(8,128)(2,1)} %near_hbm.1, s32[1,192]{1,0:T(1,128)} %bitcast.26, s32[1,192]{1,0:T(1,128)} %bitcast.27, s32[1,1]{1,0:T(1,128)} %bitcast.21.ncount_hbm, bf16[512,128]{1,0:T(8,128)(2,1)} %bitcast.22, ...), custom_call_target="tpu_custom_call" | custom-call | tf_op jit(solution)/shard_map/pallas_call | solution.py:366
  49.0 1.4 %fusion = (f32[16,128]{1,0:T(8,128)}, f32[16,128]{1,0:T(8,128)}) fusion(f32[4,16,128]{2,1,0:T(8,128)} %shard_map.122), kind=kLoop, calls=%fused_computation.1 | loop fusion | flops 8192 | bytes 49152 | tf_op jit(solution)/shard_map/sub | solution.py:435

commit v3 on v2

--- a/solution.py
+++ b/solution.py
@@ -2,6 +2,7 @@
 
 import jax
 import jax.numpy as jnp
+import numpy as np
 from jax import lax
 from jax.experimental import pallas as pl
 from jax.experimental.pallas import tpu as pltpu
@@ -26,7 +27,26 @@
     key=lambda s: (-bin(s[0]).count("1"), s[0], s[1]),
 )
 GRAY = (0, 1, 3, 2)
-FIRST = 44
+SHORT = 2
+PLANE = sorted(range(1, 16), key=lambda o: -min(o // 4, 4 - o // 4) - min(o % 4, 4 - o % 4))
+FIRST = 48
+NEXT = 6
+PLACE = {step: i for i, step in enumerate(STEPS)}
+BACK = [
+    PLACE[(sum((0, 2, 1, 3)[code >> shift & 3] << shift for shift in (0, 2, 4)), core)] for code, core in STEPS
+]
+
+
+def order_table():
+    steps = STEPS + [(0, 0)]
+    table = np.zeros((8, N * (ROWS + 4)), np.int32)
+    for i, (code, core) in enumerate(steps):
+        for part in (slice(i * ROWS, (i + 1) * ROWS), slice(N * ROWS + i * 4, N * ROWS + (i + 1) * 4)):
+            table[0, part] = GRAY[code // 16]
+            table[1, part] = core
+            table[2, part] = GRAY[code // 4 % 4]
+            table[3, part] = GRAY[code % 4]
+    return table
 
 
 def partners():
@@ -72,11 +92,11 @@
 
 
 def kernel(
-    rs_hbm, diag_hbm, near_hbm, nrow_hbm, ncol_hbm, ncount_hbm, basis_hbm, coup_hbm, frow_hbm, fcol_hbm, frank_hbm,
+    rs_hbm, diag_hbm, near_hbm, nrow_hbm, ncol_hbm, ncount_hbm, basis_hbm, coup_hbm, frow_hbm, fcol_hbm, frank_hbm, table_hbm,
     out_ref,
-    rs_ref, diag_ref, nrow_ref, ncol_ref, ncount_ref, basis_ref, frow_ref, fcol_ref, frank_ref,
+    rs_ref, diag_ref, nrow_ref, ncol_ref, ncount_ref, basis_ref, frow_ref, fcol_ref, frank_ref, table_ref,
     near, coup, coup_t, big, t8, e2_t, basis_t, hrow, hrow_t, gmask, jmask, hnr, hnc, hnr_t, hnc_t, meta,
-    gath, grow, backs, fwds, c4s, send, recv, win, spout, spin, last_out, last_in,
+    big4, t4, pick4, send4, recv4, sum_out, sum_a, sum_mid, sum_b, tree_s, tree_r, gath, grow, backs, fwds, c4s, send, recv, win, spout, spin, last_out, last_in,
     dma_sem, ssem, rsem, wsem_s, wsem_r, psem_s, psem_r, lsem_s, lsem_r,
 ):
     me = lax.axis_index(AXES)
@@ -85,7 +105,7 @@
     load_near = pltpu.make_async_copy(near_hbm, near, dma_sem.at[1])
     pairs = (
         (frow_hbm, frow_ref), (fcol_hbm, fcol_ref), (frank_hbm, frank_ref), (nrow_hbm, nrow_ref), (ncol_hbm, ncol_ref),
-        (ncount_hbm, ncount_ref), (rs_hbm, rs_ref), (basis_hbm, basis_ref), (diag_hbm, diag_ref),
+        (ncount_hbm, ncount_ref), (rs_hbm, rs_ref), (basis_hbm, basis_ref), (diag_hbm, diag_ref), (table_hbm, table_ref),
     )
     loads = [pltpu.make_async_copy(a, b, dma_sem.at[2 + i]) for i, (a, b) in enumerate(pairs)]
     for load in loads:
@@ -126,7 +146,13 @@
     hrow[...] = ones_where(iota((1, CL), 1) == frow_c)
     hrow_t[...] = ones_where(iota((CL, 1), 0) == frow)
     code_g = owner_c * ROWS + local_c // 4
-    big[pl.ds(0, FAR), :] = ones_where(iota((1, N * ROWS), 1) == code_g)
+    gx, gy, gz = lax.axis_index("gx"), lax.axis_index("gy"), lax.axis_index("gz")
+    t4[:, 0:N] = ones_where(iota((N * 4, N), 0) // 4 == iota((N * 4, N), 1))
+    steps = table_ref[...]
+    source = (
+        (gx // 2 + steps[0:1]) % 4 * 32 + (gx % 2 + steps[1:2]) % 2 * 16 + (gy + steps[2:3]) % 4 * 4 + (gz + steps[3:4]) % 4
+    )
+    big[pl.ds(0, FAR), :] = ones_where(source[:, 0 : N * ROWS] * ROWS + iota((1, N * ROWS), 1) % ROWS == code_g)
     code_s = owner * ROWS + 4 + place // 4
     t8[...] = ones_where(iota((N * ROWS, 1), 0) == code_s)
     e2_t[...] = ones_where(iota((R * R, M), 0) // R == iota((R * R, M), 1) % R)
@@ -161,6 +187,13 @@
     own = iota((CL, CL * R), 1) // R == iota((CL, CL * R), 0)
     rows_of = ones_where(iota((ROWS, CL), 1) // 4 == iota((ROWS, CL), 0))
     even = iota((NEAR, 1), 0) % 2 == 0
+    even_pair = iota((NEAR, 1), 0) % 4 < 2
+
+    def four_blocks(k):
+        first = near[pl.ds(k, 2)].reshape(2 * M, M)
+        second = near[pl.ds(k + 2, 2)].reshape(2 * M, M)
+        return jnp.concatenate([first, second], axis=1)
+
     pair_of_row = iota((16, 1), 0) // 2
     odd_row = iota((16, 1), 0) % 2 == 1
 
@@ -184,6 +217,14 @@
 
     for t in range(ITERS):
         low = field.astype(BF16)
+        if t >= SHORT:
+            sum_out[t - SHORT] = jnp.where(lane == 0, rw, jnp.where(lane == 1, ww, 0.0))
+            sum_a[t - SHORT, 0] = sum_out[t - SHORT]
+            for o in PLANE:
+                pltpu.make_async_remote_copy(
+                    sum_out.at[t - SHORT], sum_a.at[t - SHORT, o], tree_s.at[t - SHORT, 0], tree_r.at[t - SHORT, 0],
+                    device_id=gx * 16 + (gy + o // 4) % 4 * 4 + (gz + o % 4) % 4, device_id_type=LOGICAL,
+                ).start()
         win[t, 1] = low
         if t == 0:
             pl.semaphore_wait(barrier, N - 1)
@@ -198,7 +239,8 @@
 
         raw = jnp.where(own, dot(low, basis_t[...]), 0.0)
         coeffs = (raw[:, 0:M] + raw[:, M : 2 * M] + raw[:, 2 * M : 3 * M] + raw[:, 3 * M : 4 * M]).astype(BF16)
-        wide = dot(hrow[...], copies(coeffs.astype(F32)).astype(BF16)).astype(BF16)
+        four = copies(coeffs.astype(F32))
+        wide = dot(hrow[...], four.astype(BF16)).astype(BF16)
         if t == 0:
             for i in range(4):
                 part = pl.ds(i * 128, 128)
@@ -208,37 +250,47 @@
         else:
             prods = coup_t[...] * jnp.concatenate([wide] * 8, axis=1)
             c4s[...] = (dot(prods, e2_t[...]) * jmask[...]).astype(BF16)
-        tile = dot(rows_of, coeffs) + sums_tile
-        message = dot(t8[...], c4s[...])
-        if t == 0:
-            message = message + meta[...]
-        send[t] = (message.reshape(N, ROWS, M) + tile[None]).astype(BF16)
-        recv[t, me] = send[t, me]
+        if t < SHORT:
+            message = dot(t8[...], c4s[...])
+            tile = dot(rows_of, coeffs) + sums_tile
+            if t == 0:
+                message = message + meta[...]
+            send[t] = (message.reshape(N, ROWS, M) + tile[None]).astype(BF16)
+            recv[t, N - 1] = send[t, me]
+        else:
+            spread4 = jnp.concatenate([jnp.where(lane // R == q, four, 0.0) for q in range(4)] + [jnp.zeros((64, M), F32)], axis=0)
+            message = dot(t4[...], c4s[...]) + dot(pick4[...], spread4.astype(BF16))
+            send4[t - SHORT] = message.reshape(N, 4, M).astype(BF16)
+            recv4[t - SHORT, N - 1] = send4[t - SHORT, N - 1]
 
         grow_t = dot(hnr[...], low)
         zero = jnp.zeros_like(grow_t)
         grow[...] = jnp.concatenate([jnp.where(even, grow_t, zero), jnp.where(even, zero, grow_t)], axis=1).astype(BF16)
 
-        def far_copy(there, t=t):
-            return pltpu.make_async_remote_copy(
-                send.at[t, there], recv.at[t, me], ssem.at[t], rsem.at[t], device_id=there, device_id_type=LOGICAL
-            )
-
-        for there in others[:FIRST]:
-            far_copy(there).start()
+        def far_send(i, t=t):
+            there = others[i]
+            if t < SHORT:
+                src, dst = send.at[t, there], recv.at[t, BACK[i]]
+            else:
+                src, dst = send4.at[t - SHORT, i], recv4.at[t - SHORT, BACK[i]]
+            pltpu.make_async_remote_copy(
+                src, dst, ssem.at[t], rsem.at[t], device_id=there, device_id_type=LOGICAL
+            ).start()
+
+        for i in range(N - 1):
+            far_send(i)
 
         if t == 0:
             load_near.wait()
 
         def near_back(i, carry):
-            for there in others[FIRST + 7 * i : FIRST + 7 * i + 7]:
-                far_copy(there).start()
             part = pl.ds(i * 16, 16)
             lhs = grow[part, :]
             out = jnp.zeros((16, M), F32)
-            for j in range(8):
-                block = near[pl.ds(i * 16 + 2 * j, 2)].reshape(2 * M, M)
-                out = jnp.where(pair_of_row == j, dot(lhs, block), out)
+            for j in range(4):
+                out_j = dot(lhs, four_blocks(i * 16 + 4 * j))
+                out = jnp.where(pair_of_row == 2 * j, out_j[:, :M], out)
+                out = jnp.where(pair_of_row == 2 * j + 1, out_j[:, M:], out)
             backs[part, :] = out
             return carry
 
@@ -256,44 +308,83 @@
         )
         spill_prev.start()
         spill_next.start()
+        if t >= SHORT:
+            landed = sum_a.at[t - SHORT, pl.ds(1, 15)]
+            pltpu.make_async_copy(landed, landed, tree_r.at[t - SHORT, 0]).wait()
+            sum_mid[t - SHORT] = jnp.sum(sum_a[t - SHORT], axis=0)
+            sum_b[t - SHORT, 0] = sum_mid[t - SHORT]
+            for o in (4, 5, 2, 3, 6, 7, 1):
+                pltpu.make_async_remote_copy(
+                    sum_mid.at[t - SHORT], sum_b.at[t - SHORT, o], tree_s.at[t - SHORT, 1], tree_r.at[t - SHORT, 1],
+                    device_id=(gx + o) % 8 * 16 + gy * 4 + gz, device_id_type=LOGICAL,
+                ).start()
+        if t == SHORT - 1:
+            numbers = dot(t4[:, 0 : N], recv[0].astype(F32)[:, 7, :].astype(BF16))
+            row4 = iota((N * 4, 1), 0) % 4
+            numbers = jnp.where(row4 % 2 == 0, numbers, pltpu.roll(numbers, M - 4, 1))
+            spread = ones_where((iota((M, M), 0) == iota((M, M), 1) // CL) & (iota((M, M), 0) < 4))
+            numbers = dot(numbers.astype(BF16), spread)
+            hot = jnp.where((iota((1, M), 1) % CL).astype(F32) == numbers, 1.0, 0.0)
+            hot = jnp.where(iota((1, M), 1) < 64, hot, 0.0)
+            pick4[...] = jnp.where(row4 < 2, hot, 0.0).astype(BF16)
+            big4[pl.ds(FAR, 64), :] = jnp.transpose(jnp.where(row4 >= 2, hot, 0.0))[0:64, :].astype(BF16)
+            source4 = source[:, N * ROWS :]
+            col4 = iota((1, N * 4), 1) % 4
+            big4[pl.ds(0, FAR), :] = ones_where(source4 * 4 + col4 == owner_c * 4 + place_c // 4)
+            source4_c = jnp.transpose(jnp.broadcast_to(source4.astype(F32), (8, N * 4)))[:, 0:1].astype(jnp.int32)
+            t4[...] = ones_where(source4_c * 4 + row4 == owner * 4 + 2 + place // 4)
 
         to_next.wait_recv()
         to_prev.wait_recv()
-        gath[...] = dot(hnc[...], win[t].reshape(3 * CL, M)).astype(BF16)
+        gath_t = dot(hnc[...], win[t].reshape(3 * CL, M))
+        gath[...] = jnp.concatenate(
+            [jnp.where(even_pair, gath_t, zero), jnp.where(even_pair, zero, gath_t)], axis=1
+        ).astype(BF16)
 
         def near_forward(i, carry):
-            part = pl.ds(pl.multiple_of(i * 16, 16), 16)
+            part = pl.ds(i * 16, 16)
             lhs = gath[part, :]
             out = jnp.zeros((16, M), F32)
-            for j in range(8):
-                block = near[pl.ds(pl.multiple_of(i * 16 + 2 * j, 2), 2)].reshape(2 * M, M)
-                got = dot_t(lhs, block)
+            for j in range(4):
+                got = dot_t(lhs, four_blocks(i * 16 + 4 * j))
                 got = jnp.where(odd_row, got[:, M:], got[:, :M])
-                out = jnp.where(pair_of_row == j, got, out)
+                out = jnp.where(pair_of_row // 2 == j, got, out)
             fwds[part, :] = out
             return carry
 
-        lax.fori_loop(0, 12, near_forward, 0)
+        for i in range(12):
+            near_forward(i, 0)
         hi, lo = split(fwds[...])
         product = diag_ref[...] * field + spilled[CL : 2 * CL] + dot(hnr_t[...], hi) + dot(hnr_t[...], lo)
 
-        everyone = recv.at[t, pl.ds(0, N - 1)]
-        pltpu.make_async_copy(everyone, everyone, rsem.at[t]).wait()
-        arrived = recv[t].reshape(N * ROWS, M)
-        if t == 0:
-            pick = ones_where(iota((16, M), 1) == iota((16, M), 0))
-            numbers = dot_t(pick, arrived)
-            col = iota((1, N * ROWS), 1) % ROWS
-            first = jnp.concatenate([numbers[:, 3:], numbers[:, :3]], axis=1)
-            second = jnp.concatenate([numbers[:, 2:], numbers[:, :2]], axis=1)
-            pieces = []
-            for q in range(4):
-                number = jnp.where(col == 4, first[q : q + 1], jnp.where(col == 5, second[4 + q : 5 + q], -1.0))
-                pieces.append(ones_where(iota((CL, 1), 0).astype(F32) == number))
-            big[pl.ds(FAR, 64), :] = jnp.concatenate(pieces, axis=0)
-        got = dot(big[...], arrived)
-        totals = got[FAR + 64 : FAR + 65, :]
-        c4s[...] = copies(got[0:FAR] * gmask[...]).astype(BF16)
+        if t < SHORT:
+            landed = recv.at[t, pl.ds(0, N - 1)]
+            pltpu.make_async_copy(landed, landed, rsem.at[t]).wait()
+            arrived = recv[t].reshape(N * ROWS, M)
+            if t == 0:
+                pick = ones_where(iota((16, M), 1) == iota((16, M), 0))
+                numbers = dot_t(pick, arrived)
+                col = iota((1, N * ROWS), 1) % ROWS
+                first = jnp.concatenate([numbers[:, 3:], numbers[:, :3]], axis=1)
+                second = jnp.concatenate([numbers[:, 2:], numbers[:, :2]], axis=1)
+                pieces = []
+                for q in range(4):
+                    number = jnp.where(col == 4, first[q : q + 1], jnp.where(col == 5, second[4 + q : 5 + q], -1.0))
+                    pieces.append(ones_where(iota((CL, 1), 0).astype(F32) == number))
+                big[pl.ds(FAR, 64), :] = jnp.concatenate(pieces, axis=0)
+            got = dot(big[...], arrived)
+            totals = got[FAR + 64 : FAR + 65, :]
+            totals = totals + pltpu.roll(totals, M - 1, 1) + pltpu.roll(totals, M - 2, 1)
+            rw, ww = totals[:, 0:1], totals[:, 3:4]
+        else:
+            landed = recv4.at[t - SHORT, pl.ds(0, N - 1)]
+            pltpu.make_async_copy(landed, landed, rsem.at[t]).wait()
+            got = dot(big4[...], recv4[t - SHORT].reshape(N * 4, M))
+            landed = sum_b.at[t - SHORT, pl.ds(1, 7)]
+            pltpu.make_async_copy(landed, landed, tree_r.at[t - SHORT, 1]).wait()
+            totals = jnp.sum(sum_b[t - SHORT], axis=0)
+            rw, ww = totals[:, 0:1], totals[:, 1:2]
+        c4s[...] = copies(got[0:FAR] * (gmask if t < SHORT else jmask)[...]).astype(BF16)
         if t == 0:
             z = jnp.zeros((CL, R * R), F32)
             for i in range(4):
@@ -321,15 +412,15 @@
         if t == 0:
             image = product
         else:
-            rw = totals[:, 0:1] + totals[:, 1:2] + totals[:, 2:3]
-            ww = totals[:, 3:4] + totals[:, 4:5] + totals[:, 5:6]
             step = rw / (ww + EPS)
             solution = solution + step * residual
             residual = residual - step * image
             image = image - step * product
         field = image
         if t + 1 < ITERS:
-            sums_tile = to_rows(whole(residual * image), whole(image * image))
+            rw, ww = whole(residual * image), whole(image * image)
+            if t + 1 < SHORT:
+                sums_tile = to_rows(rw, ww)
 
     rw, ww = whole(residual * image), whole(image * image)
     last_out[...] = jnp.where(lane == 0, rw, jnp.where(lane == 1, ww, 0.0))
@@ -349,8 +440,13 @@
     out_ref[3] = jnp.broadcast_to(step, (CL, M))
 
     pltpu.make_async_copy(everyone, everyone, lsem_s).wait()
+    for t in range(ITERS - SHORT):
+        sent = sum_a.at[t, pl.ds(1, 15)]
+        pltpu.make_async_copy(sent, sent, tree_s.at[t, 0]).wait()
+        sent = sum_b.at[t, pl.ds(1, 7)]
+        pltpu.make_async_copy(sent, sent, tree_s.at[t, 1]).wait()
     for t in range(ITERS):
-        sent = send.at[t, pl.ds(0, N - 1)]
+        sent = send.at[t, pl.ds(0, N - 1)] if t < SHORT else send4.at[t - SHORT, pl.ds(0, N - 1)]
         pltpu.make_async_copy(sent, sent, ssem.at[t]).wait()
         for i in range(2):
             pltpu.make_async_copy(win.at[t, 1], win.at[t, 1], wsem_s.at[t, i]).wait()
@@ -366,7 +462,7 @@
     out = pl.pallas_call(
         kernel,
         out_shape=jax.ShapeDtypeStruct((4, CL, M), F32),
-        in_specs=[hbm] * 11,
+        in_specs=[hbm] * 12,
         out_specs=vmem,
         scratch_shapes=[
             v((CL, M), F32),
@@ -378,6 +474,7 @@
             v((1, FAR), ints),
             v((1, FAR), ints),
             v((1, FAR), ints),
+            v((8, N * (ROWS + 4)), ints),
             v((NEAR, M, M), BF16),
             v((FAR, R * R), BF16),
             v((FAR, R * R), BF16),
@@ -394,19 +491,30 @@
             v((CL, NEAR), BF16),
             v((3 * CL, NEAR), BF16),
             v((N * ROWS, M), F32),
-            v((NEAR, M), BF16),
+            v((FAR + 64, N * 4), BF16),
+            v((N * 4, FAR), BF16),
+            v((N * 4, M), BF16),
+            v((ITERS - SHORT, N, 4, M), BF16),
+            v((ITERS - SHORT, N, 4, M), BF16),
+            v((ITERS - SHORT, 1, M), F32),
+            v((ITERS - SHORT, 16, 1, M), F32),
+            v((ITERS - SHORT, 1, M), F32),
+            v((ITERS - SHORT, 8, 1, M), F32),
+            dma((ITERS - SHORT, 2)),
+            dma((ITERS - SHORT, 2)),
+            v((NEAR, 2 * M), BF16),
             v((NEAR, 2 * M), BF16),
             v((NEAR, M), F32),
             v((NEAR, M), F32),
             v((FAR, M), BF16),
-            v((ITERS, N, ROWS, M), BF16),
-            v((ITERS, N, ROWS, M), BF16),
+            v((SHORT, N, ROWS, M), BF16),
+            v((SHORT, N, ROWS, M), BF16),
             v((ITERS, 3, CL, M), BF16),
             v((ITERS, 2, CL, M), F32),
             v((ITERS, 2, CL, M), F32),
             v((1, M), F32),
             v((N, 1, M), F32),
-            dma((11,)),
+            dma((12,)),
             dma((ITERS,)),
             dma((ITERS,)),
             dma((ITERS, 2)),
@@ -431,6 +539,7 @@
         frow.reshape(1, FAR),
         fcol.reshape(1, FAR),
         frank.reshape(1, FAR),
+        jnp.asarray(order_table()),
     )
     return out[0] + out[3] * out[1], out[1] - out[3] * out[2]
 

time: 50.5 us -> 49.2 us (0.974)
  Pallas kernels: 47.7 us -> 46.4 us
    pallas_call x1, Pallas kernels: 47.7 us -> 46.4 us  [on_device(): pl.pallas_call(kernel, out_shape=jax.ShapeDtypeStruct((4, CL, M), F32), i...]
where the time goes in v3:
time: 49.2 us; the launch traced here: 49 us
  Pallas kernels  46.4 us (94%)
  other arithmetic  1.36 us (3%)
  between operations  1.29 us (3%)
    pallas_call x1, Pallas kernels, on_device(): pl.pallas_call(kernel, out_shape=jax.ShapeDtypeStruct((4, CL, M), F32), i...  46.4 us
    sub x1, other arithmetic, on_device(): return (out[0] + out[3] * out[1], out[1] - out[3] * out[2])  1.36 us

profile of v3, /device:TPU:1, one launch (start us, length us, event | category | flops | bytes accessed | tf_op | source)
XLA Modules:
  0.0 49.0 jit_solution(11535966205249677420)
XLA Ops:
  1.3 46.4 %shard_map.131 = f32[4,16,128]{2,1,0:T(8,128)} custom-call(f32[16,128]{1,0:T(8,128)} %rs_hbm.1, f32[16,128]{1,0:T(8,128)} %diag_hbm.1, bf16[192,128,128]{2,1,0:T(8,128)(2,1)} %near_hbm.1, s32[1,192]{1,0:T(1,128)} %bitcast.26, s32[1,192]{1,0:T(1,128)} %bitcast.27, s32[1,1]{1,0:T(1,128)} %bitcast.21.ncount_hbm, bf16[512,128]{1,0:T(8,128)(2,1)} %bitcast.22, ...), custom_call_target="tpu_custom_call" | custom-call | tf_op jit(solution)/shard_map/pallas_call | solution.py:462
  47.7 1.4 %fusion = (f32[16,128]{1,0:T(8,128)}, f32[16,128]{1,0:T(8,128)}) fusion(f32[4,16,128]{2,1,0:T(8,128)} %shard_map.131), kind=kLoop, calls=%fused_computation.1 | loop fusion | flops 8192 | bytes 49152 | tf_op jit(solution)/shard_map/sub | solution.py:544

commit v4 on v3

--- a/solution.py
+++ b/solution.py
@@ -27,7 +27,7 @@
     key=lambda s: (-bin(s[0]).count("1"), s[0], s[1]),
 )
 GRAY = (0, 1, 3, 2)
-SHORT = 2
+SHORT = 1
 PLANE = sorted(range(1, 16), key=lambda o: -min(o // 4, 4 - o // 4) - min(o % 4, 4 - o % 4))
 FIRST = 48
 NEXT = 6
@@ -96,7 +96,7 @@
     out_ref,
     rs_ref, diag_ref, nrow_ref, ncol_ref, ncount_ref, basis_ref, frow_ref, fcol_ref, frank_ref, table_ref,
     near, coup, coup_t, big, t8, e2_t, basis_t, hrow, hrow_t, gmask, jmask, hnr, hnc, hnr_t, hnc_t, meta,
-    big4, t4, pick4, send4, recv4, sum_out, sum_a, sum_mid, sum_b, tree_s, tree_r, gath, grow, backs, fwds, c4s, send, recv, win, spout, spin, last_out, last_in,
+    big4, t4, pick4, repeat4, send4, recv4, sum_out, sum_a, sum_mid, sum_b, tree_s, tree_r, gath, grow, backs, fwds, c4s, send, recv, win, spout, spin, last_out, last_in,
     dma_sem, ssem, rsem, wsem_s, wsem_r, psem_s, psem_r, lsem_s, lsem_r,
 ):
     me = lax.axis_index(AXES)
@@ -147,12 +147,17 @@
     hrow_t[...] = ones_where(iota((CL, 1), 0) == frow)
     code_g = owner_c * ROWS + local_c // 4
     gx, gy, gz = lax.axis_index("gx"), lax.axis_index("gy"), lax.axis_index("gz")
-    t4[:, 0:N] = ones_where(iota((N * 4, N), 0) // 4 == iota((N * 4, N), 1))
+    repeat4[...] = ones_where(iota((N * 4, N), 0) // 4 == iota((N * 4, N), 1))
     steps = table_ref[...]
     source = (
         (gx // 2 + steps[0:1]) % 4 * 32 + (gx % 2 + steps[1:2]) % 2 * 16 + (gy + steps[2:3]) % 4 * 4 + (gz + steps[3:4]) % 4
     )
     big[pl.ds(0, FAR), :] = ones_where(source[:, 0 : N * ROWS] * ROWS + iota((1, N * ROWS), 1) % ROWS == code_g)
+    source4 = source[:, N * ROWS :]
+    big4[pl.ds(0, FAR), :] = ones_where(source4 * 4 + iota((1, N * 4), 1) % 4 == owner_c * 4 + place_c // 4)
+    source4_c = jnp.transpose(jnp.broadcast_to(source4.astype(F32), (8, N * 4)))[:, 0:1].astype(jnp.int32)
+    row4 = iota((N * 4, 1), 0) % 4
+    t4[...] = ones_where(source4_c * 4 + row4 == owner * 4 + 2 + place // 4)
     code_s = owner * ROWS + 4 + place // 4
     t8[...] = ones_where(iota((N * ROWS, 1), 0) == code_s)
     e2_t[...] = ones_where(iota((R * R, M), 0) // R == iota((R * R, M), 1) % R)
@@ -161,9 +166,6 @@
     code_m = owner * ROWS + 7
     t7 = ones_where(iota((N * ROWS, 1), 0) == code_m)
     meta[...] = dot(t7, jnp.where(lane == place_c, local_c.astype(F32), 0.0).astype(BF16))
-    big[pl.ds(FAR + 64, 16), :] = ones_where(
-        (iota((16, N * ROWS), 0) == 0) & (iota((16, N * ROWS), 1) % ROWS == 6)
-    )
     count = ncount_ref[0, 0]
     live = iota((1, NEAR), 1) < count
     nrow = nrow_ref[...] - me * CL
@@ -200,20 +202,7 @@
     field = rs_ref[...]
     residual = field
     solution = jnp.zeros_like(field)
-    sums_tile = jnp.zeros((ROWS, M), F32)
-    sub8 = iota((ROWS, M), 0)
-    lane8 = iota((ROWS, M), 1)
     image = field
-
-    def to_rows(rw, ww):
-        tile = jnp.zeros((ROWS, M), F32)
-        for i, value in enumerate((rw, ww)):
-            rest = jnp.broadcast_to(value, (ROWS, M))
-            for part in range(3):
-                piece = rest.astype(BF16).astype(F32)
-                rest = rest - piece
-                tile = tile + jnp.where((sub8 == 6) & (lane8 == 3 * i + part), piece, 0.0)
-        return tile
 
     for t in range(ITERS):
         low = field.astype(BF16)
@@ -252,7 +241,7 @@
             c4s[...] = (dot(prods, e2_t[...]) * jmask[...]).astype(BF16)
         if t < SHORT:
             message = dot(t8[...], c4s[...])
-            tile = dot(rows_of, coeffs) + sums_tile
+            tile = dot(rows_of, coeffs)
             if t == 0:
                 message = message + meta[...]
             send[t] = (message.reshape(N, ROWS, M) + tile[None]).astype(BF16)
@@ -318,21 +307,6 @@
                     sum_mid.at[t - SHORT], sum_b.at[t - SHORT, o], tree_s.at[t - SHORT, 1], tree_r.at[t - SHORT, 1],
                     device_id=(gx + o) % 8 * 16 + gy * 4 + gz, device_id_type=LOGICAL,
                 ).start()
-        if t == SHORT - 1:
-            numbers = dot(t4[:, 0 : N], recv[0].astype(F32)[:, 7, :].astype(BF16))
-            row4 = iota((N * 4, 1), 0) % 4
-            numbers = jnp.where(row4 % 2 == 0, numbers, pltpu.roll(numbers, M - 4, 1))
-            spread = ones_where((iota((M, M), 0) == iota((M, M), 1) // CL) & (iota((M, M), 0) < 4))
-            numbers = dot(numbers.astype(BF16), spread)
-            hot = jnp.where((iota((1, M), 1) % CL).astype(F32) == numbers, 1.0, 0.0)
-            hot = jnp.where(iota((1, M), 1) < 64, hot, 0.0)
-            pick4[...] = jnp.where(row4 < 2, hot, 0.0).astype(BF16)
-            big4[pl.ds(FAR, 64), :] = jnp.transpose(jnp.where(row4 >= 2, hot, 0.0))[0:64, :].astype(BF16)
-            source4 = source[:, N * ROWS :]
-            col4 = iota((1, N * 4), 1) % 4
-            big4[pl.ds(0, FAR), :] = ones_where(source4 * 4 + col4 == owner_c * 4 + place_c // 4)
-            source4_c = jnp.transpose(jnp.broadcast_to(source4.astype(F32), (8, N * 4)))[:, 0:1].astype(jnp.int32)
-            t4[...] = ones_where(source4_c * 4 + row4 == owner * 4 + 2 + place // 4)
 
         to_next.wait_recv()
         to_prev.wait_recv()
@@ -373,9 +347,14 @@
                     pieces.append(ones_where(iota((CL, 1), 0).astype(F32) == number))
                 big[pl.ds(FAR, 64), :] = jnp.concatenate(pieces, axis=0)
             got = dot(big[...], arrived)
-            totals = got[FAR + 64 : FAR + 65, :]
-            totals = totals + pltpu.roll(totals, M - 1, 1) + pltpu.roll(totals, M - 2, 1)
-            rw, ww = totals[:, 0:1], totals[:, 3:4]
+            numbers = dot(repeat4[...], recv[0].astype(F32)[:, 7, :].astype(BF16))
+            numbers = jnp.where(row4 % 2 == 0, numbers, pltpu.roll(numbers, M - 4, 1))
+            spread = ones_where((iota((M, M), 0) == iota((M, M), 1) // CL) & (iota((M, M), 0) < 4))
+            numbers = dot(numbers.astype(BF16), spread)
+            hot = jnp.where((iota((1, M), 1) % CL).astype(F32) == numbers, 1.0, 0.0)
+            hot = jnp.where(iota((1, M), 1) < 64, hot, 0.0)
+            pick4[...] = jnp.where(row4 < 2, hot, 0.0).astype(BF16)
+            big4[pl.ds(FAR, 64), :] = jnp.transpose(jnp.where(row4 >= 2, hot, 0.0))[0:64, :].astype(BF16)
         else:
             landed = recv4.at[t - SHORT, pl.ds(0, N - 1)]
             pltpu.make_async_copy(landed, landed, rsem.at[t]).wait()
@@ -419,8 +398,6 @@
         field = image
         if t + 1 < ITERS:
             rw, ww = whole(residual * image), whole(image * image)
-            if t + 1 < SHORT:
-                sums_tile = to_rows(rw, ww)
 
     rw, ww = whole(residual * image), whole(image * image)
     last_out[...] = jnp.where(lane == 0, rw, jnp.where(lane == 1, ww, 0.0))
@@ -478,7 +455,7 @@
             v((NEAR, M, M), BF16),
             v((FAR, R * R), BF16),
             v((FAR, R * R), BF16),
-            v((FAR + 80, N * ROWS), BF16),
+            v((FAR + 64, N * ROWS), BF16),
             v((N * ROWS, FAR), BF16),
             v((R * R, M), BF16),
             v((M, CL * R), BF16),
@@ -494,6 +471,7 @@
             v((FAR + 64, N * 4), BF16),
             v((N * 4, FAR), BF16),
             v((N * 4, M), BF16),
+            v((N * 4, N), BF16),
             v((ITERS - SHORT, N, 4, M), BF16),
             v((ITERS - SHORT, N, 4, M), BF16),
             v((ITERS - SHORT, 1, M), F32),

time: 49.2 us -> 48.2 us (0.980)
  Pallas kernels: 46.4 us -> 45.3 us
    pallas_call x1, Pallas kernels: 46.4 us -> 45.3 us  [on_device(): pl.pallas_call(kernel, out_shape=jax.ShapeDtypeStruct((4, CL, M), F32), i...]
where the time goes in v4:
time: 48.2 us; the launch traced here: 48 us
  Pallas kernels  45.3 us (94%)
  other arithmetic  1.36 us (3%)
  between operations  1.29 us (3%)
    pallas_call x1, Pallas kernels, on_device(): pl.pallas_call(kernel, out_shape=jax.ShapeDtypeStruct((4, CL, M), F32), i...  45.3 us
    sub x1, other arithmetic, on_device(): return (out[0] + out[3] * out[1], out[1] - out[3] * out[2])  1.36 us

profile of v4, /device:TPU:1, one launch (start us, length us, event | category | flops | bytes accessed | tf_op | source)
XLA Modules:
  0.0 48.0 jit_solution(6630604408970779513)
XLA Ops:
  1.3 45.3 %shard_map.131 = f32[4,16,128]{2,1,0:T(8,128)} custom-call(f32[16,128]{1,0:T(8,128)} %rs_hbm.1, f32[16,128]{1,0:T(8,128)} %diag_hbm.1, bf16[192,128,128]{2,1,0:T(8,128)(2,1)} %near_hbm.1, s32[1,192]{1,0:T(1,128)} %bitcast.26, s32[1,192]{1,0:T(1,128)} %bitcast.27, s32[1,1]{1,0:T(1,128)} %bitcast.21.ncount_hbm, bf16[512,128]{1,0:T(8,128)(2,1)} %bitcast.22, ...), custom_call_target="tpu_custom_call" | custom-call | tf_op jit(solution)/shard_map/pallas_call | solution.py:439
  46.6 1.4 %fusion = (f32[16,128]{1,0:T(8,128)}, f32[16,128]{1,0:T(8,128)}) fusion(f32[4,16,128]{2,1,0:T(8,128)} %shard_map.131), kind=kLoop, calls=%fused_computation.1 | loop fusion | flops 8192 | bytes 49152 | tf_op jit(solution)/shard_map/sub | solution.py:522

commit v5 on v4

--- a/solution.py
+++ b/solution.py
@@ -141,23 +141,8 @@
     place_c = jnp.transpose(jnp.broadcast_to(place_f, (8, FAR)))[:, 0:1].astype(jnp.int32)
 
     lane = iota((1, M), 1)
-    gmask[...] = jnp.where(lane // R == local_c % 4, 1.0, 0.0)
     jmask[...] = jnp.where(lane // R == place_c % 4, 1.0, 0.0)
     hrow[...] = ones_where(iota((1, CL), 1) == frow_c)
-    hrow_t[...] = ones_where(iota((CL, 1), 0) == frow)
-    code_g = owner_c * ROWS + local_c // 4
-    gx, gy, gz = lax.axis_index("gx"), lax.axis_index("gy"), lax.axis_index("gz")
-    repeat4[...] = ones_where(iota((N * 4, N), 0) // 4 == iota((N * 4, N), 1))
-    steps = table_ref[...]
-    source = (
-        (gx // 2 + steps[0:1]) % 4 * 32 + (gx % 2 + steps[1:2]) % 2 * 16 + (gy + steps[2:3]) % 4 * 4 + (gz + steps[3:4]) % 4
-    )
-    big[pl.ds(0, FAR), :] = ones_where(source[:, 0 : N * ROWS] * ROWS + iota((1, N * ROWS), 1) % ROWS == code_g)
-    source4 = source[:, N * ROWS :]
-    big4[pl.ds(0, FAR), :] = ones_where(source4 * 4 + iota((1, N * 4), 1) % 4 == owner_c * 4 + place_c // 4)
-    source4_c = jnp.transpose(jnp.broadcast_to(source4.astype(F32), (8, N * 4)))[:, 0:1].astype(jnp.int32)
-    row4 = iota((N * 4, 1), 0) % 4
-    t4[...] = ones_where(source4_c * 4 + row4 == owner * 4 + 2 + place // 4)
     code_s = owner * ROWS + 4 + place // 4
     t8[...] = ones_where(iota((N * ROWS, 1), 0) == code_s)
     e2_t[...] = ones_where(iota((R * R, M), 0) // R == iota((R * R, M), 1) % R)
@@ -166,17 +151,7 @@
     code_m = owner * ROWS + 7
     t7 = ones_where(iota((N * ROWS, 1), 0) == code_m)
     meta[...] = dot(t7, jnp.where(lane == place_c, local_c.astype(F32), 0.0).astype(BF16))
-    count = ncount_ref[0, 0]
-    live = iota((1, NEAR), 1) < count
-    nrow = nrow_ref[...] - me * CL
-    ncol = ncol_ref[...] - me * CL + CL
-    hnr_t[...] = ones_where((iota((CL, 1), 0) == nrow) & live)
-    hnc_t[...] = ones_where((iota((3 * CL, 1), 0) == ncol) & live)
-    ncodes = jnp.concatenate([nrow.astype(F32), ncol.astype(F32), jnp.zeros((6, NEAR), F32)], axis=0)
-    ncodes_t = jnp.transpose(ncodes)
-    hnr[...] = ones_where(iota((1, CL), 1) == ncodes_t[:, 0:1].astype(jnp.int32))
-    hnc[...] = ones_where(iota((1, 3 * CL), 1) == ncodes_t[:, 1:2].astype(jnp.int32))
-
+    row4 = iota((N * 4, 1), 0) % 4
     load_coup.wait()
     ab = iota((1, R * R), 1)
     top = jnp.maximum(ab // R, ab % R)
@@ -215,16 +190,15 @@
                     device_id=gx * 16 + (gy + o // 4) % 4 * 4 + (gz + o % 4) % 4, device_id_type=LOGICAL,
                 ).start()
         win[t, 1] = low
-        if t == 0:
-            pl.semaphore_wait(barrier, N - 1)
         to_next = pltpu.make_async_remote_copy(
             win.at[t, 1], win.at[t, 0], wsem_s.at[t, 0], wsem_r.at[t, 0], device_id=nxt, device_id_type=LOGICAL
         )
         to_prev = pltpu.make_async_remote_copy(
             win.at[t, 1], win.at[t, 2], wsem_s.at[t, 1], wsem_r.at[t, 1], device_id=prv, device_id_type=LOGICAL
         )
-        to_next.start()
-        to_prev.start()
+        if t > 0:
+            to_next.start()
+            to_prev.start()
 
         raw = jnp.where(own, dot(low, basis_t[...]), 0.0)
         coeffs = (raw[:, 0:M] + raw[:, M : 2 * M] + raw[:, 2 * M : 3 * M] + raw[:, 3 * M : 4 * M]).astype(BF16)
@@ -252,10 +226,6 @@
             send4[t - SHORT] = message.reshape(N, 4, M).astype(BF16)
             recv4[t - SHORT, N - 1] = send4[t - SHORT, N - 1]
 
-        grow_t = dot(hnr[...], low)
-        zero = jnp.zeros_like(grow_t)
-        grow[...] = jnp.concatenate([jnp.where(even, grow_t, zero), jnp.where(even, zero, grow_t)], axis=1).astype(BF16)
-
         def far_send(i, t=t):
             there = others[i]
             if t < SHORT:
@@ -266,8 +236,41 @@
                 src, dst, ssem.at[t], rsem.at[t], device_id=there, device_id_type=LOGICAL
             ).start()
 
+        if t == 0:
+            pl.semaphore_wait(barrier, N - 1)
+            to_next.start()
+            to_prev.start()
         for i in range(N - 1):
             far_send(i)
+        if t == 0:
+            gmask[...] = jnp.where(lane // R == local_c % 4, 1.0, 0.0)
+            hrow_t[...] = ones_where(iota((CL, 1), 0) == frow)
+            code_g = owner_c * ROWS + local_c // 4
+            gx, gy, gz = lax.axis_index("gx"), lax.axis_index("gy"), lax.axis_index("gz")
+            repeat4[...] = ones_where(iota((N * 4, N), 0) // 4 == iota((N * 4, N), 1))
+            steps = table_ref[...]
+            source = (
+                (gx // 2 + steps[0:1]) % 4 * 32 + (gx % 2 + steps[1:2]) % 2 * 16 + (gy + steps[2:3]) % 4 * 4 + (gz + steps[3:4]) % 4
+            )
+            big[pl.ds(0, FAR), :] = ones_where(source[:, 0 : N * ROWS] * ROWS + iota((1, N * ROWS), 1) % ROWS == code_g)
+            source4 = source[:, N * ROWS :]
+            big4[pl.ds(0, FAR), :] = ones_where(source4 * 4 + iota((1, N * 4), 1) % 4 == owner_c * 4 + place_c // 4)
+            source4_c = jnp.transpose(jnp.broadcast_to(source4.astype(F32), (8, N * 4)))[:, 0:1].astype(jnp.int32)
+            t4[...] = ones_where(source4_c * 4 + row4 == owner * 4 + 2 + place // 4)
+            count = ncount_ref[0, 0]
+            live = iota((1, NEAR), 1) < count
+            nrow = nrow_ref[...] - me * CL
+            ncol = ncol_ref[...] - me * CL + CL
+            hnr_t[...] = ones_where((iota((CL, 1), 0) == nrow) & live)
+            hnc_t[...] = ones_where((iota((3 * CL, 1), 0) == ncol) & live)
+            ncodes = jnp.concatenate([nrow.astype(F32), ncol.astype(F32), jnp.zeros((6, NEAR), F32)], axis=0)
+            ncodes_t = jnp.transpose(ncodes)
+            hnr[...] = ones_where(iota((1, CL), 1) == ncodes_t[:, 0:1].astype(jnp.int32))
+            hnc[...] = ones_where(iota((1, 3 * CL), 1) == ncodes_t[:, 1:2].astype(jnp.int32))
+        grow_t = dot(hnr[...], low)
+        zero = jnp.zeros_like(grow_t)
+        grow[...] = jnp.concatenate([jnp.where(even, grow_t, zero), jnp.where(even, zero, grow_t)], axis=1).astype(BF16)
+
 
         if t == 0:
             load_near.wait()
@@ -371,7 +374,7 @@
                 c4 = c4s[part, :].astype(F32)
                 hi, lo = split(coup[part, :].astype(F32) * jnp.concatenate([c4] * 8, axis=1))
                 rows = hrow_t[:, i * 128 : (i + 1) * 128]
-                z = z + dot(rows, hi) + dot(rows, lo)
+                z = z + dot(jnp.concatenate([rows, rows], axis=1), jnp.concatenate([hi, lo], axis=0))
         else:
             z = dot(hrow_t[...], coup[...] * jnp.concatenate([c4s[...]] * 8, axis=1))
         hi, lo = split(z)
@@ -407,16 +410,6 @@
         pltpu.make_async_remote_copy(
             last_out, last_in.at[me], lsem_s, lsem_r, device_id=there, device_id_type=LOGICAL
         ).start()
-    everyone = last_in.at[pl.ds(0, N - 1)]
-    pltpu.make_async_copy(everyone, everyone, lsem_r).wait()
-    totals = jnp.sum(last_in[...], axis=0)
-    step = totals[:, 0:1] / (totals[:, 1:2] + EPS)
-    out_ref[0] = solution
-    out_ref[1] = residual
-    out_ref[2] = image
-    out_ref[3] = jnp.broadcast_to(step, (CL, M))
-
-    pltpu.make_async_copy(everyone, everyone, lsem_s).wait()
     for t in range(ITERS - SHORT):
         sent = sum_a.at[t, pl.ds(1, 15)]
         pltpu.make_async_copy(sent, sent, tree_s.at[t, 0]).wait()
@@ -428,6 +421,16 @@
         for i in range(2):
             pltpu.make_async_copy(win.at[t, 1], win.at[t, 1], wsem_s.at[t, i]).wait()
             pltpu.make_async_copy(spout.at[t, i], spout.at[t, i], psem_s.at[t, i]).wait()
+    everyone = last_in.at[pl.ds(0, N - 1)]
+    pltpu.make_async_copy(everyone, everyone, lsem_r).wait()
+    totals = jnp.sum(last_in[...], axis=0)
+    step = totals[:, 0:1] / (totals[:, 1:2] + EPS)
+    out_ref[0] = solution
+    out_ref[1] = residual
+    out_ref[2] = image
+    out_ref[3] = jnp.broadcast_to(step, (CL, M))
+
+    pltpu.make_async_copy(everyone, everyone, lsem_s).wait()
 
 
 def on_device(rs, diag, near, nrow, ncol, ncount, basis, coup, frow, fcol, frank):

time: 48.2 us -> 47.4 us (0.983)
  Pallas kernels: 45.3 us -> 44.6 us
    pallas_call x1, Pallas kernels: 45.3 us -> 44.6 us  [on_device(): pl.pallas_call(kernel, out_shape=jax.ShapeDtypeStruct((4, CL, M), F32), i...]
where the time goes in v5:
time: 47.4 us; the launch traced here: 47.3 us
  Pallas kernels  44.6 us (94%)
  other arithmetic  1.36 us (3%)
  between operations  1.29 us (3%)
    pallas_call x1, Pallas kernels, on_device(): pl.pallas_call(kernel, out_shape=jax.ShapeDtypeStruct((4, CL, M), F32), i...  44.6 us
    sub x1, other arithmetic, on_device(): return (out[0] + out[3] * out[1], out[1] - out[3] * out[2])  1.36 us

profile of v5, /device:TPU:1, one launch (start us, length us, event | category | flops | bytes accessed | tf_op | source)
XLA Modules:
  0.0 47.3 jit_solution(8028511486789101723)
XLA Ops:
  1.3 44.6 %shard_map.131 = f32[4,16,128]{2,1,0:T(8,128)} custom-call(f32[16,128]{1,0:T(8,128)} %rs_hbm.1, f32[16,128]{1,0:T(8,128)} %diag_hbm.1, bf16[192,128,128]{2,1,0:T(8,128)(2,1)} %near_hbm.1, s32[1,192]{1,0:T(1,128)} %bitcast.26, s32[1,192]{1,0:T(1,128)} %bitcast.27, s32[1,1]{1,0:T(1,128)} %bitcast.21.ncount_hbm, bf16[512,128]{1,0:T(8,128)(2,1)} %bitcast.22, ...), custom_call_target="tpu_custom_call" | custom-call | tf_op jit(solution)/shard_map/pallas_call | solution.py:442
  45.9 1.4 %fusion = (f32[16,128]{1,0:T(8,128)}, f32[16,128]{1,0:T(8,128)}) fusion(f32[4,16,128]{2,1,0:T(8,128)} %shard_map.131), kind=kLoop, calls=%fused_computation.1 | loop fusion | flops 8192 | bytes 49152 | tf_op jit(solution)/shard_map/sub | solution.py:525

commit v6 on v5

--- a/solution.py
+++ b/solution.py
@@ -148,9 +148,7 @@
     e2_t[...] = ones_where(iota((R * R, M), 0) // R == iota((R * R, M), 1) % R)
     eye = ones_where(iota((M, M), 0) == iota((M, M), 1))
     basis_t[...] = dot_t(eye, basis_ref[...]).astype(BF16)
-    code_m = owner * ROWS + 7
-    t7 = ones_where(iota((N * ROWS, 1), 0) == code_m)
-    meta[...] = dot(t7, jnp.where(lane == place_c, local_c.astype(F32), 0.0).astype(BF16))
+    meta[...] = (jmask[...] * local_c.astype(F32)).astype(BF16)
     row4 = iota((N * 4, 1), 0) % 4
     load_coup.wait()
     ab = iota((1, R * R), 1)
@@ -214,10 +212,9 @@
             prods = coup_t[...] * jnp.concatenate([wide] * 8, axis=1)
             c4s[...] = (dot(prods, e2_t[...]) * jmask[...]).astype(BF16)
         if t < SHORT:
-            message = dot(t8[...], c4s[...])
+            both = dot(t8[...], jnp.concatenate([c4s[...], meta[...]], axis=1))
+            message = both[:, :M] + pltpu.roll(both[:, M:], 2, 0)
             tile = dot(rows_of, coeffs)
-            if t == 0:
-                message = message + meta[...]
             send[t] = (message.reshape(N, ROWS, M) + tile[None]).astype(BF16)
             recv[t, N - 1] = send[t, me]
         else:
@@ -247,7 +244,7 @@
             hrow_t[...] = ones_where(iota((CL, 1), 0) == frow)
             code_g = owner_c * ROWS + local_c // 4
             gx, gy, gz = lax.axis_index("gx"), lax.axis_index("gy"), lax.axis_index("gz")
-            repeat4[...] = ones_where(iota((N * 4, N), 0) // 4 == iota((N * 4, N), 1))
+            repeat4[...] = ones_where(iota((N * 4, 2 * N), 0) // 4 + iota((N * 4, 2 * N), 0) % 2 * N == iota((N * 4, 2 * N), 1))
             steps = table_ref[...]
             source = (
                 (gx // 2 + steps[0:1]) % 4 * 32 + (gx % 2 + steps[1:2]) % 2 * 16 + (gy + steps[2:3]) % 4 * 4 + (gz + steps[3:4]) % 4
@@ -339,20 +336,20 @@
             pltpu.make_async_copy(landed, landed, rsem.at[t]).wait()
             arrived = recv[t].reshape(N * ROWS, M)
             if t == 0:
-                pick = ones_where(iota((16, M), 1) == iota((16, M), 0))
+                pick = ones_where(iota((16, M), 1) == iota((16, M), 0) * R)
                 numbers = dot_t(pick, arrived)
                 col = iota((1, N * ROWS), 1) % ROWS
-                first = jnp.concatenate([numbers[:, 3:], numbers[:, :3]], axis=1)
-                second = jnp.concatenate([numbers[:, 2:], numbers[:, :2]], axis=1)
+                numbers = jnp.concatenate([numbers[:, 2:], numbers[:, :2]], axis=1)
                 pieces = []
                 for q in range(4):
-                    number = jnp.where(col == 4, first[q : q + 1], jnp.where(col == 5, second[4 + q : 5 + q], -1.0))
+                    number = jnp.where((col == 4) | (col == 5), numbers[q : q + 1], -1.0)
                     pieces.append(ones_where(iota((CL, 1), 0).astype(F32) == number))
                 big[pl.ds(FAR, 64), :] = jnp.concatenate(pieces, axis=0)
             got = dot(big[...], arrived)
-            numbers = dot(repeat4[...], recv[0].astype(F32)[:, 7, :].astype(BF16))
-            numbers = jnp.where(row4 % 2 == 0, numbers, pltpu.roll(numbers, M - 4, 1))
-            spread = ones_where((iota((M, M), 0) == iota((M, M), 1) // CL) & (iota((M, M), 0) < 4))
+            rows = recv[0].astype(F32)
+            rows = jnp.concatenate([rows[:, 6, :], rows[:, 7, :]], axis=0).astype(BF16)
+            numbers = dot(repeat4[...], rows)
+            spread = ones_where(iota((M, M), 0) == iota((M, M), 1) // CL * R)
             numbers = dot(numbers.astype(BF16), spread)
             hot = jnp.where((iota((1, M), 1) % CL).astype(F32) == numbers, 1.0, 0.0)
             hot = jnp.where(iota((1, M), 1) < 64, hot, 0.0)
@@ -470,11 +467,11 @@
             v((NEAR, 3 * CL), BF16),
             v((CL, NEAR), BF16),
             v((3 * CL, NEAR), BF16),
-            v((N * ROWS, M), F32),
+            v((FAR, M), BF16),
             v((FAR + 64, N * 4), BF16),
             v((N * 4, FAR), BF16),
             v((N * 4, M), BF16),
-            v((N * 4, N), BF16),
+            v((N * 4, 2 * N), BF16),
             v((ITERS - SHORT, N, 4, M), BF16),
             v((ITERS - SHORT, N, 4, M), BF16),
             v((ITERS - SHORT, 1, M), F32),

time: 47.4 us -> 47.3 us (level)
  no operation moved by 1% of the time
where the time goes in v6:
time: 47.3 us; the launch traced here: 47.1 us
  Pallas kernels  44.4 us (94%)
  other arithmetic  1.36 us (3%)
  between operations  1.29 us (3%)
    pallas_call x1, Pallas kernels, on_device(): pl.pallas_call(kernel, out_shape=jax.ShapeDtypeStruct((4, CL, M), F32), i...  44.4 us
    sub x1, other arithmetic, on_device(): return (out[0] + out[3] * out[1], out[1] - out[3] * out[2])  1.36 us

profile of v6, /device:TPU:1, one launch (start us, length us, event | category | flops | bytes accessed | tf_op | source)
XLA Modules:
  0.0 47.1 jit_solution(9545389653317866819)
XLA Ops:
  1.3 44.4 %shard_map.131 = f32[4,16,128]{2,1,0:T(8,128)} custom-call(f32[16,128]{1,0:T(8,128)} %rs_hbm.1, f32[16,128]{1,0:T(8,128)} %diag_hbm.1, bf16[192,128,128]{2,1,0:T(8,128)(2,1)} %near_hbm.1, s32[1,192]{1,0:T(1,128)} %bitcast.26, s32[1,192]{1,0:T(1,128)} %bitcast.27, s32[1,1]{1,0:T(1,128)} %bitcast.21.ncount_hbm, bf16[512,128]{1,0:T(8,128)(2,1)} %bitcast.22, ...), custom_call_target="tpu_custom_call" | custom-call | tf_op jit(solution)/shard_map/pallas_call | solution.py:439
  45.7 1.4 %fusion = (f32[16,128]{1,0:T(8,128)}, f32[16,128]{1,0:T(8,128)}) fusion(f32[4,16,128]{2,1,0:T(8,128)} %shard_map.131), kind=kLoop, calls=%fused_computation.1 | loop fusion | flops 8192 | bytes 49152 | tf_op jit(solution)/shard_map/sub | solution.py:522

commit v7 on v6

--- a/solution.py
+++ b/solution.py
@@ -207,7 +207,8 @@
                 part = pl.ds(i * 128, 128)
                 prods = coup_t[part, :].astype(F32) * jnp.concatenate([wide[i * 128 : (i + 1) * 128].astype(F32)] * 8, axis=1)
                 hi, lo = split(prods)
-                c4s[part, :] = ((dot(hi, e2_t[...]) + dot(lo, e2_t[...])) * jmask[part, :]).astype(BF16)
+                pair = dot(jnp.concatenate([hi, lo], axis=0), e2_t[...])
+                c4s[part, :] = ((pair[:128] + pair[128:]) * jmask[part, :]).astype(BF16)
         else:
             prods = coup_t[...] * jnp.concatenate([wide] * 8, axis=1)
             c4s[...] = (dot(prods, e2_t[...]) * jmask[...]).astype(BF16)

time: 47.3 us -> 47.3 us (level)
  no operation moved by 1% of the time
where the time goes in v7:
time: 47.3 us; the launch traced here: 47.2 us
  Pallas kernels  44.5 us (94%)
  other arithmetic  1.36 us (3%)
  between operations  1.29 us (3%)
    pallas_call x1, Pallas kernels, on_device(): pl.pallas_call(kernel, out_shape=jax.ShapeDtypeStruct((4, CL, M), F32), i...  44.5 us
    sub x1, other arithmetic, on_device(): return (out[0] + out[3] * out[1], out[1] - out[3] * out[2])  1.36 us

profile of v7, /device:TPU:1, one launch (start us, length us, event | category | flops | bytes accessed | tf_op | source)
XLA Modules:
  0.0 47.2 jit_solution(6547309867341397470)
XLA Ops:
  1.3 44.5 %shard_map.131 = f32[4,16,128]{2,1,0:T(8,128)} custom-call(f32[16,128]{1,0:T(8,128)} %rs_hbm.1, f32[16,128]{1,0:T(8,128)} %diag_hbm.1, bf16[192,128,128]{2,1,0:T(8,128)(2,1)} %near_hbm.1, s32[1,192]{1,0:T(1,128)} %bitcast.26, s32[1,192]{1,0:T(1,128)} %bitcast.27, s32[1,1]{1,0:T(1,128)} %bitcast.21.ncount_hbm, bf16[512,128]{1,0:T(8,128)(2,1)} %bitcast.22, ...), custom_call_target="tpu_custom_call" | custom-call | tf_op jit(solution)/shard_map/pallas_call | solution.py:440
  45.8 1.4 %fusion = (f32[16,128]{1,0:T(8,128)}, f32[16,128]{1,0:T(8,128)}) fusion(f32[4,16,128]{2,1,0:T(8,128)} %shard_map.131), kind=kLoop, calls=%fused_computation.1 | loop fusion | flops 8192 | bytes 49152 | tf_op jit(solution)/shard_map/sub | solution.py:523
